TPU v7x, 512 devices: a whole 4x8x8 slice. The times are simulated.
512 devices in a mesh: kvp: 16 (over z, core), section: 4 (over x), tp: 8 (over y).
Axes of the slice: x: 4, y: 8, z: 8, core: 2. Of those that a mesh axis runs over, the one named last changes fastest.
Arguments:
- span: bfloat16 [4, 128, 8192], P('section', 'tp', 'kvp'), may hold values from -64 to 64
- gain: float32 [4, 8192], P('section', 'kvp'), may hold values from 0.1 to 1.9
- w_query: bfloat16 [4, 8192, 8192], P('section', 'kvp', 'tp'), may hold values from -0.0625 to 0.0625
- keys: bfloat16 [4, 65536, 8, 128], P('section', 'kvp', 'tp'), may hold values from -220 to 220
- values: bfloat16 [4, 65536, 8, 128], P('section', 'kvp', 'tp'), may hold values from -8 to 8
- lengths: int32 [16], P('kvp'), may hold values from 1 to 4096, as said below
- w_out: bfloat16 [4, 8192, 8192], P('section', 'tp', 'kvp'), may hold values from -0.0625 to 0.0625
Outputs:
- next_span: bfloat16 [4, 128, 8192], P('section', 'tp', 'kvp')
Inputs may be any that keep to these rules, and one draw needn't show every extreme that they name: `lengths`: every shard but the last holds 4096 valid positions; the last holds 1 to 4096.
All inputs are finite; a program needn't handle non-finite values.
Results may differ from a plain program's by a relative error of at most 0.02.
Values may be sent and summed in bfloat16 or wider, within the bound.
No kernel may reach another device: no remote copies, remote signals or barrier semaphores. Data moves between devices by JAX's collectives and lax.ppermute only.
A program may use at most 64 MiB of HBM per device.

v0:
```python
import math

import jax
import jax.numpy as jnp
from jax import lax
from jax.sharding import PartitionSpec as P

D = 8192
HEADS = 64
KV_HEADS = 8
BLOCK = 512


EPS = 1e-05
NEG = -1e30


def from_behind(value, axis, steps):
    count = lax.axis_size(axis)
    pairs = [(source, (source + steps) % count) for source in range(count)]
    return lax.ppermute(value, axis, pairs)


def combine_pair(first, second):
    best = jnp.maximum(first[0], second[0])
    left = jnp.exp(first[0] - best)
    right = jnp.exp(second[0] - best)
    total = first[1] * left + second[1] * right
    accum = first[2] * left[..., None] + second[2] * right[..., None]
    return (best, total, accum)


def local(span, gain, w_query, keys, values, lengths, w_out):
    rows = lax.all_gather(span[0], "tp", axis=0, tiled=True)
    wide = rows.astype(jnp.float32)
    square = lax.psum(jnp.sum(wide * wide, axis=1), "kvp")
    normed = (wide * lax.rsqrt(square / D + EPS)[:, None] * gain[0][None, :]).astype(jnp.bfloat16)
    weight_query = w_query[0]
    query = lax.psum(
        jnp.dot(normed, weight_query, preferred_element_type=jnp.float32), "kvp"
    ).astype(jnp.bfloat16)
    cache_keys = keys[0]
    cache_values = values[0]
    count = cache_keys.shape[0]
    key_heads = cache_keys.shape[1]
    head_dim = cache_keys.shape[2]
    group = HEADS // KV_HEADS
    tokens = query.shape[0]
    query_heads = query.reshape(tokens, key_heads, group, head_dim)
    valid = lengths[0]
    block = BLOCK
    blocks = count // block
    scale = 1.0 / math.sqrt(head_dim)

    def block_step(index, carry):
        start = index * block
        key_block = lax.dynamic_slice_in_dim(cache_keys, start, block, 0)
        value_block = lax.dynamic_slice_in_dim(cache_values, start, block, 0)
        scores = (
            jnp.einsum("tghd,jgd->ghtj", query_heads, key_block, preferred_element_type=jnp.float32)
            * scale
        )
        inside = start + jnp.arange(block) < valid
        scores = jnp.where(inside, scores, NEG)
        top = jnp.max(scores, axis=3)
        probs = jnp.where(inside, jnp.exp(scores - top[..., None]), 0.0).astype(jnp.bfloat16)
        total = jnp.sum(probs.astype(jnp.float32), axis=3)
        accum = jnp.einsum("ghtj,jgd->ghtd", probs, value_block, preferred_element_type=jnp.float32)
        return combine_pair(carry, (top, total, accum))

    start_carry = (
        jnp.full((key_heads, group, tokens), NEG, jnp.float32),
        jnp.zeros((key_heads, group, tokens), jnp.float32),
        jnp.zeros((key_heads, group, tokens, head_dim), jnp.float32),
    )
    local_top, local_total, local_accum = lax.fori_loop(0, blocks, block_step, start_carry)
    width = key_heads * group * head_dim
    tops, totals, accums = (
        lax.all_gather(local_top[None], "kvp", axis=0, tiled=True),
        lax.all_gather(local_total[None], "kvp", axis=0, tiled=True),
        lax.all_gather(local_accum[None], "kvp", axis=0, tiled=True),
    )
    best = jnp.max(tops, axis=0)
    factor = jnp.exp(tops - best[None])
    denom = jnp.sum(totals * factor, axis=0)
    numer = jnp.sum(accums * factor[..., None], axis=0)
    attended = (numer / denom[..., None]).astype(jnp.bfloat16)
    attended = jnp.transpose(attended, (2, 0, 1, 3)).reshape(tokens, width)
    weight_out = w_out[0]
    projected = lax.psum_scatter(
        jnp.dot(attended, weight_out, preferred_element_type=jnp.float32).astype(jnp.bfloat16),
        "tp",
        scatter_dimension=0,
        tiled=True,
    ).astype(jnp.float32)
    updated = (projected + span[0].astype(jnp.float32)).astype(jnp.bfloat16)
    moved = from_behind(updated, "section", 1)
    return moved[None]


def solution(mesh):
    in_specs = (
        P("section", "tp", "kvp"),
        P("section", "kvp"),
        P("section", "kvp", "tp"),
        P("section", "kvp", "tp", None),
        P("section", "kvp", "tp", None),
        P("kvp"),
        P("section", "tp", "kvp"),
    )
    out_specs = P("section", "tp", "kvp")
    return jax.shard_map(local, mesh=mesh, in_specs=in_specs, out_specs=out_specs, check_vma=False)
```

profile of v0, /device:TPU:8, one launch (start us, length us, event | category | flops | bytes accessed | tf_op | source)
XLA Modules:
  0.0 269.5 jit_solution(3681718068086068372)
XLA Ops:
  6.5 27.6 %all-gather = bf16[1,128,512]{2,1,0:T(8,128)(2,1)S(1)} all-gather(bf16[1,16,512]{2,1,0:T(8,128)(2,1)} %param.9), channel_id=2, replica_groups=mesh['kvp'=16,'section'=4,'tp'=8] {'tp'}, dimensions={1}, use_global_device_ids=true | all-gather | bytes 147456 | tf_op jit(solution)/shard_map/all_gather | solution.py:34
  34.2 27.4 %psum.14 = f32[128]{0:T(128)S(1)} all-reduce(f32[128]{0:T(128)S(1)} %fusion.27), channel_id=1, replica_groups=mesh['kvp'=16,'section'=4,'tp'=8] {'kvp'}, use_global_device_ids=true, to_apply=%region_1.0 | all-reduce | flops 128 | bytes 1024 | tf_op jit(solution)/shard_map/psum | solution.py:36
  61.6 1.0 fusion.24
  62.7 51.3 %all-reduce.1 = bf16[128,1024]{1,0:T(8,128)(2,1)S(1)} all-reduce(f32[128,1024]{1,0:T(8,128)S(1)} %fusion.24), channel_id=1, replica_groups=mesh['kvp'=16,'section'=4,'tp'=8] {'kvp'}, use_global_device_ids=true, to_apply=%region_2.0 | all-reduce | flops 131072 | bytes 786432 | tf_op jit(solution)/shard_map/psum | solution.py:39
  114.1 38.6 %while.18 = (s32[]{:T(128)}, f32[1,8,128]{2,1,0:T(8,128)S(1)}, f32[1,8,128]{2,1,0:T(8,128)S(1)}, f32[1,8,128,128]{3,2,1,0:T(8,128)S(1)}, s32[]{:T(128)}, /*index...) while((s32[]{:T(128)}, f32[1,8,128]{2,1,0:T(8,128)S(1)}, ...), condition=%wide.region_6.7_spmd.clone, body=%wide.region_3.6_spmd.clone.sunk | while | flops 276833280 | bytes 7944903 | solution.py:76
  114.1 0.7 add_compare_fusion.2
  114.7 1.4 bitcast_reduce_fusion.2
  116.1 0.6 convert_reduce_fusion.2
  116.8 2.1 fusion.49
  118.9 0.7 add_compare_fusion.2
  119.6 1.4 bitcast_reduce_fusion.2
  120.9 0.6 convert_reduce_fusion.2
  121.6 2.1 fusion.49
  123.7 0.7 add_compare_fusion.2
  124.4 1.4 bitcast_reduce_fusion.2
  125.8 0.6 convert_reduce_fusion.2
  126.4 2.1 fusion.49
  128.6 0.7 add_compare_fusion.2
  129.2 1.4 bitcast_reduce_fusion.2
  130.6 0.6 convert_reduce_fusion.2
  131.3 2.1 fusion.49
  133.4 0.7 add_compare_fusion.2
  134.1 1.4 bitcast_reduce_fusion.2
  135.4 0.6 convert_reduce_fusion.2
  136.1 2.1 fusion.49
  138.2 0.7 add_compare_fusion.2
  138.9 1.4 bitcast_reduce_fusion.2
  140.3 0.6 convert_reduce_fusion.2
  140.9 2.1 fusion.49
  143.1 0.7 add_compare_fusion.2
  143.7 1.4 bitcast_reduce_fusion.2
  145.1 0.6 convert_reduce_fusion.2
  145.7 2.1 fusion.49
  147.9 0.7 add_compare_fusion.2
  148.5 1.4 bitcast_reduce_fusion.2
  149.9 0.6 convert_reduce_fusion.2
  150.6 2.1 fusion.49
  152.7 0.8 copy-done.2
  153.6 14.3 %all-gather.2 = f32[16,8,128]{2,1,0:T(8,128)S(1)} all-gather(f32[1,8,128]{2,1,0:T(8,128)S(1)} %get-tuple-element.147), channel_id=4, replica_groups=mesh['kvp'=16,'section'=4,'tp'=8] {'kvp'}, dimensions={0}, use_global_device_ids=true | all-gather | bytes 69632 | tf_op jit(solution)/shard_map/all_gather | solution.py:79
  168.0 16.4 %all-gather.3 = f32[16,8,128]{2,1,0:T(8,128)S(1)} all-gather(f32[1,8,128]{2,1,0:T(8,128)S(1)} %get-tuple-element.148), channel_id=5, replica_groups=mesh['kvp'=16,'section'=4,'tp'=8] {'kvp'}, dimensions={0}, use_global_device_ids=true | all-gather | bytes 69632 | tf_op jit(solution)/shard_map/all_gather | solution.py:80
  184.4 26.8 %all-gather.6.cloned.1.call-done = f32[16,8,128,128]{3,2,1,0:T(8,128)} async-done(((f32[1,8,128,128]{3,2,1,0:T(8,128)}), f32[16,8,128,128]{3,2,1,0:T(8,128)}) %all-gather.6.cloned.1.call-update) | async-done | bytes 8388624 | tf_op jit(solution)/shard_map/all_gather | solution.py:81
  211.2 5.3 %fusion.22 = f32[8,128,128]{2,1,0:T(8,128)S(1)} fusion(f32[16,8,128,128]{3,2,1,0:T(8,128)} %all-gather.6.cloned.1.call-done, f32[16,8,128]{2,1,0:T(8,128)S(1)} %get-tuple-element.222), kind=kLoop, calls=%fused_computation.34 | loop fusion | flops 4063232 | bytes 8978432 | tf_op jit(solution)/shard_map/reduce_sum | solution.py:86
  217.0 1.0 convolution_convert_fusion
  218.0 36.5 %reduce-scatter.2.cloned.1.call-done = bf16[16,512]{1,0:T(8,128)(2,1)} async-done(((bf16[128,512]{1,0:T(8,128)(2,1)}), bf16[16,512]{1,0:T(8,128)(2,1)}) %reduce-scatter.2.cloned.1.call-update) | async-done | bytes 16400 | tf_op jit(solution)/shard_map/reduce_scatter | solution.py:90
  254.5 0.7 fusion.38
  255.2 3.4 %collective-permute-start = (bf16[16,512]{1,0:T(8,128)(2,1)S(1)}, bf16[16,512]{1,0:T(8,128)(2,1)S(1)}, u32[]{:S(2)}, u32[]{:S(2)}) collective-permute-start(bf16[16,512]{1,0:T(8,128)(2,1)S(1)} %fusion.38), channel_id=1, source_target_pairs={{0,8},{8,16},{16,24},{24,0},{1,9},{9,17},{17,25},{25,1},{2,10},{10... | collective-permute-start | bytes 49160 | tf_op jit(solution)/shard_map/ppermute | solution.py:21
  258.6 3.4 %collective-permute-done = bf16[16,512]{1,0:T(8,128)(2,1)S(1)} collective-permute-done((bf16[16,512]{1,0:T(8,128)(2,1)S(1)}, bf16[16,512]{1,0:T(8,128)(2,1)S(1)}, u32[]{:S(2)}, u32[]{:S(2)}) %collective-permute-start) | collective-permute-done | bytes 16416 | tf_op jit(solution)/shard_map/ppermute | solution.py:21
  262.0 0.6 copy.32
  (46 shorter events, 0.9 us)
Async XLA Ops:
  6.5 55.1 %copy-start = (bf16[1,512,1024]{2,1,0:T(8,128)(2,1)S(1)}, bf16[1,512,1024]{2,1,0:T(8,128)(2,1)}, u32[]{:S(2)}) copy-start(bf16[1,512,1024]{2,1,0:T(8,128)(2,1)} %param.11) | copy-start | bytes 3145732
  6.5 204.7 %all-gather.6.cloned.1.call-start = ((), (), s32[]{:S(2)}) async-start(), calls=%async_computation.2 | async-start | bytes 8912896 | tf_op jit(solution)/shard_map/all_gather | solution.py:81
  152.7 0.8 copy-start.2
  153.6 100.9 %reduce-scatter.2.cloned.1.call-start = ((), (), s32[]{:S(2)}) async-start(), calls=%async_computation.1 | async-start | bytes 147456 | tf_op jit(solution)/shard_map/reduce_scatter | solution.py:90
  211.2 5.8 %copy-start.1 = (bf16[1,1024,512]{2,1,0:T(8,128)(2,1)S(1)}, bf16[1,1024,512]{2,1,0:T(8,128)(2,1)}, u32[]{:S(2)}) copy-start(bf16[1,1024,512]{2,1,0:T(8,128)(2,1)} %param.15) | copy-start | bytes 3145732
  216.6 37.9 %copy-start.3 = (bf16[1,16,512]{2,1,0:T(8,128)(2,1)S(1)}, bf16[1,16,512]{2,1,0:T(8,128)(2,1)}, u32[]{:S(2)}) copy-start(bf16[1,16,512]{2,1,0:T(8,128)(2,1)} %param.9) | copy-start | bytes 49156
  255.2 6.8 %collective-permute-start = (bf16[16,512]{1,0:T(8,128)(2,1)S(1)}, bf16[16,512]{1,0:T(8,128)(2,1)S(1)}, u32[]{:S(2)}, u32[]{:S(2)}) collective-permute-start(bf16[16,512]{1,0:T(8,128)(2,1)S(1)} %fusion.38), channel_id=1, source_target_pairs={{0,8},{8,16},{16,24},{24,0},{1,9},{9,17},{17,25},{25,1},{2,10},{10... | collective-permute-start | bytes 49160 | tf_op jit(solution)/shard_map/ppermute | solution.py:21
Sparse Core Ops, SparseCore 0:
  153.7 57.4 all-gather.5
  218.1 36.3 reduce-scatter.1
where the time goes:
time: 270 us; the launch traced here: 269 us
  blocking collectives  137 us (51%)
  waiting for transfers between devices  66.8 us (25%)
  matrix products  29.9 us (11%)
  other arithmetic  16.6 us (6%)
  between operations  13.5 us (5%)
  starting transfers between devices  3.46 us (1%)
    psum x1, blocking collectives, local(): lax.psum(jnp.dot(normed, weight_query, preferred_element_type=jnp.float32...  51.3 us
    reduce_scatter x1, waiting for transfers between devices, local(): lax.psum_scatter(jnp.dot(attended, weight_out, preferred_element_type=jnp...  36.5 us
    all_gather x1, blocking collectives, local(): rows = lax.all_gather(span[0], 'tp', axis=0, tiled=True)  27.6 us
    psum x1, blocking collectives, local(): square = lax.psum(jnp.sum(wide * wide, axis=1), 'kvp')  27.4 us
    all_gather x1, waiting for transfers between devices, local(): lax.all_gather(local_accum[None], 'kvp', axis=0, tiled=True)  26.8 us
    dot_general x8, matrix products, block_step(): jnp.einsum('ghtj,jgd->ghtd', probs, value_block, preferred_element_type=j...  17 us
    all_gather x1, blocking collectives, local(): lax.all_gather(local_total[None], 'kvp', axis=0, tiled=True)  16.4 us
    all_gather x1, blocking collectives, local(): lax.all_gather(local_top[None], 'kvp', axis=0, tiled=True)  14.3 us
  transfers between devices with their start and end apart: 3, of which 3 were waited for; matrix products, arithmetic and copies ran while one was open for 0% of the time, Pallas kernels for 0%

commit v1 on v0

v1 whole, which is shorter than its diff:
```python
import functools
import math

import jax
import jax.numpy as jnp
from jax import lax
from jax.experimental import pallas as pl
from jax.experimental.pallas import tpu as pltpu
from jax.sharding import Mesh, PartitionSpec as P

D = 8192
HEADS = 64
KV_HEADS = 8
HD = 128
EPS = 1e-05

GROUP = HEADS // KV_HEADS
CORES = 2
OWN = GROUP // CORES
LANES = 128
STAT_ROWS = 8
ONES_ROWS = 16
VALUE_ROWS = HD + ONES_ROWS
PIECE = 1024

QUERY_SCALE = 128.0
ACCUM_SCALE = 4096.0
OUT_SCALE = 64.0
LEVEL_STEP = 256.0

def from_behind(value, axis, steps):
    count = lax.axis_size(axis)
    pairs = [(source, (source + steps) % count) for source in range(count)]
    return lax.ppermute(value, axis, pairs)


def spread(value, axis):
    count = lax.psum(1, axis)
    return lax.all_to_all(jnp.broadcast_to(value[None], (count,) + value.shape), axis, 0, 0)


def square_kernel(span, out):
    wide = span[...].astype(jnp.float32)
    square = jnp.sum(wide * wide, axis=1, keepdims=True)
    step = wide.shape[0]
    at = lax.broadcasted_iota(jnp.int32, (step, LANES), 0)
    lane = lax.broadcasted_iota(jnp.int32, (step, LANES), 1)
    row = jnp.sum(jnp.where(at == lane, square, 0.0), axis=0, keepdims=True)
    out[...] = jnp.broadcast_to(row[None], out.shape)


def norm_kernel(squares, span, gain, out):
    wide = span[...].astype(jnp.float32)
    step = wide.shape[0]
    row = jnp.sum(squares[...], axis=0)
    at = lax.broadcasted_iota(jnp.int32, (step, LANES), 0)
    lane = lax.broadcasted_iota(jnp.int32, (step, LANES), 1)
    square = jnp.sum(jnp.where(at == lane, row, 0.0), axis=1, keepdims=True)
    normed = (wide * lax.rsqrt(square / D + EPS) * gain[...]).astype(jnp.bfloat16)
    out[...] = jnp.broadcast_to(normed[None], out.shape)


def project_kernel(normed, weight, out, *, chips):
    width = weight.shape[1] // CORES
    step = normed.shape[0] // chips
    for core in range(CORES):
        part = jnp.dot(
            normed[...],
            weight[:, core * width : (core + 1) * width],
            preferred_element_type=jnp.float32,
        )
        out[core * chips : (core + 1) * chips] = part.reshape(chips, step, width) * QUERY_SCALE


def small_call(kernel, shape, dtype, *operands):
    return pl.pallas_call(
        kernel,
        out_shape=jax.ShapeDtypeStruct(shape, dtype),
        in_specs=[pl.BlockSpec(memory_space=pltpu.VMEM)] * len(operands),
        out_specs=pl.BlockSpec(memory_space=pltpu.VMEM),
        compiler_params=pltpu.CompilerParams(vmem_limit_bytes=8 * 1024 * 1024),
    )(*operands)


def key_row(position):
    step, at = divmod(position, PIECE)
    return step * (PIECE + VALUE_ROWS * (PIECE // LANES)) + at


def value_row(position):
    step, at = divmod(position, PIECE)
    return key_row(step * PIECE) + PIECE + at // LANES * VALUE_ROWS


def prepare_kernel(length, keys, values, after, out):
    del after
    count = keys.shape[0]
    valid = length[0]
    at = lax.broadcasted_iota(jnp.int32, (HD, HD), 0)
    lane = lax.broadcasted_iota(jnp.int32, (HD, HD), 1)
    unit = jnp.where(at == lane, 1.0, 0.0).astype(jnp.bfloat16)

    def write(masked):
        for start in range(0, count, PIECE):
            own_keys = keys[start : start + PIECE, :]
            own_values = values[start : start + PIECE, :]
            if masked:
                inside = start + lax.broadcasted_iota(jnp.int32, (PIECE, HD), 0) < valid
                first = keys[0:16, :].astype(jnp.float32)[0:1, :]
                own_keys = jnp.where(inside, own_keys.astype(jnp.float32), first)
                own_keys = own_keys.astype(jnp.bfloat16)
                own_values = jnp.where(inside, own_values.astype(jnp.float32), 0.0)
                own_values = own_values.astype(jnp.bfloat16)
            out[key_row(start) : key_row(start) + PIECE, :] = own_keys
            across = lax.dot_general(
                unit, own_values, (((1,), (1,)), ((), ())), preferred_element_type=jnp.float32
            ).astype(jnp.bfloat16)
            for block in range(0, PIECE, LANES):
                row = value_row(start + block)
                out[row : row + HD, :] = across[:, block : block + LANES]
                ones = jnp.ones((ONES_ROWS, LANES), jnp.float32)
                if masked:
                    place = lax.broadcasted_iota(jnp.int32, (ONES_ROWS, LANES), 1)
                    ones = jnp.where(start + block + place < valid, ones, 0.0)
                out[row + HD : row + VALUE_ROWS, :] = ones.astype(jnp.bfloat16)

    pl.when(valid >= count)(functools.partial(write, False))
    pl.when(valid < count)(functools.partial(write, True))


def prepare(lengths, keys, values, after):
    count = keys.shape[0]
    return pl.pallas_call(
        prepare_kernel,
        out_shape=jax.ShapeDtypeStruct((key_row(count), HD), jnp.bfloat16),
        in_specs=[
            pl.BlockSpec(memory_space=pltpu.SMEM),
            pl.BlockSpec(memory_space=pltpu.VMEM),
            pl.BlockSpec(memory_space=pltpu.VMEM),
            pl.BlockSpec(memory_space=pl.ANY),
        ],
        out_specs=pl.BlockSpec(memory_space=pltpu.VMEM),
        compiler_params=pltpu.CompilerParams(vmem_limit_bytes=16 * 1024 * 1024),
        cost_estimate=pl.CostEstimate(
            flops=8 * count * HD, bytes_accessed=8 * count * HD, transcendentals=0
        ),
    )(lengths, keys, values, after)


def attend_kernel(query, here, there, out, scores, *, chunks):
    tokens = query.shape[0]
    wide = 2 * tokens
    cache = (here, there)
    count = scores.shape[1]
    pieces = count // PIECE
    pairs = OWN // 2
    unit = math.log2(math.e) / math.sqrt(HD)

    def query_pair(pair):
        base = pair * 2 * HD
        return jnp.concatenate(
            [query[:, base : base + HD], query[:, base + HD : base + 2 * HD]], axis=0
        )

    def score_piece(number, pair_query, piece, top):
        half, pair = divmod(number, pairs)
        part = lax.dot_general(
            cache[half][key_row(piece * PIECE) : key_row(piece * PIECE) + PIECE, :],
            pair_query,
            (((1,), (1,)), ((), ())),
            preferred_element_type=jnp.float32,
        )
        scores[number % 2, piece * PIECE : (piece + 1) * PIECE, :] = part
        return jnp.maximum(top, jnp.max(part.reshape(PIECE // 8, 8, wide), axis=0))

    first = jnp.full((8, wide), -jnp.inf, jnp.float32)
    top = first
    ahead = query_pair(0)
    for piece in range(pieces):
        top = score_piece(0, ahead, piece, top)
    held = []
    for number in range(CORES * pairs):
        half, pair = divmod(number, pairs)
        best = jnp.max(top, axis=0, keepdims=True)
        top = first
        more = number + 1 < CORES * pairs
        if more:
            ahead = query_pair((number + 1) % pairs)
        accum = jnp.zeros((VALUE_ROWS, wide), jnp.float32)
        for piece in range(pieces):
            if more:
                top = score_piece(number + 1, ahead, piece, top)
            span = slice(piece * PIECE, (piece + 1) * PIECE)
            weight = jnp.exp2((scores[number % 2, span, :] - best) * unit).astype(jnp.bfloat16)
            across = [
                cache[half][value_row(start) : value_row(start) + VALUE_ROWS, :]
                for start in range(piece * PIECE, (piece + 1) * PIECE, LANES)
            ]
            accum += jnp.dot(
                jnp.concatenate(across, axis=1), weight, preferred_element_type=jnp.float32
            )
        held.append((best, accum))
        if half + 1 < CORES:
            continue

        best_here, accum_here = held[pair]
        both = jnp.maximum(best_here, best)
        accum = accum_here * jnp.exp2((best_here - both) * unit) + accum * jnp.exp2(
            (best - both) * unit
        )
        total = accum[HD : HD + 1, :]
        level = both * unit + jnp.log2(total)
        high = jnp.where(jnp.abs(level) < 1.0, 0.0, level).astype(jnp.bfloat16).astype(jnp.float32)
        rest = level - high
        middle = rest.astype(jnp.bfloat16).astype(jnp.float32)
        stats = jnp.concatenate(
            [
                high * (1.0 / LEVEL_STEP),
                middle,
                (rest - middle) * LEVEL_STEP,
                jnp.zeros((STAT_ROWS - 3, wide), jnp.float32),
            ],
            axis=0,
        )
        mean = accum[0:HD, :] * (ACCUM_SCALE / total)
        per_head = chunks // OWN
        rows = HD // per_head
        for side in range(2):
            lanes = slice(side * tokens, (side + 1) * tokens)
            for part in range(per_head):
                chunk = (2 * pair + side) * per_head + part
                out[chunk, 0:rows, :] = mean[part * rows : (part + 1) * rows, lanes]
                out[chunk, rows : rows + STAT_ROWS, :] = stats[:, lanes]


def attend(query, here, there, count, chunks):
    tokens = query.shape[0]
    rows = OWN * HD // chunks
    return pl.pallas_call(
        functools.partial(attend_kernel, chunks=chunks),
        out_shape=jax.ShapeDtypeStruct((chunks, rows + STAT_ROWS, tokens), jnp.float32),
        in_specs=[pl.BlockSpec(memory_space=pltpu.VMEM)] * 3,
        out_specs=pl.BlockSpec(memory_space=pltpu.VMEM),
        scratch_shapes=[pltpu.VMEM((2, count, 2 * tokens), jnp.float32)],
        compiler_params=pltpu.CompilerParams(vmem_limit_bytes=24 * 1024 * 1024),
        cost_estimate=pl.CostEstimate(
            flops=4 * GROUP * tokens * count * HD,
            bytes_accessed=8 * count * HD,
            transcendentals=GROUP * tokens * count,
        ),
    )(query, here, there)


def local(span, gain, w_query, keys, values, lengths, w_out):
    chips = lax.axis_size("z")
    shards = CORES * chips
    heads = lax.axis_size("tp")
    own = span[0]
    step = own.shape[0]
    tokens = heads * step
    width = GROUP * HD

    squares = small_call(square_kernel, (shards, 1, LANES), jnp.float32, own)
    here = prepare(lengths, keys[0, :, 0, :], values[0, :, 0, :], squares)
    squares = lax.all_to_all(squares, ("core", "z"), 0, 0)
    squares, here = lax.optimization_barrier((squares, here))
    there = from_behind(here, "core", 1)
    normed = small_call(norm_kernel, (heads,) + own.shape, jnp.bfloat16, squares, own, gain)
    normed = lax.all_to_all(normed, "tp", 0, 0).reshape(tokens, -1)

    partial = small_call(
        functools.partial(project_kernel, chips=chips),
        (shards, tokens // chips, width // CORES),
        jnp.float32,
        normed,
        w_query[0],
    )
    parts = lax.all_to_all(partial.astype(jnp.float16), ("core", "z"), 0, 0)
    query = jnp.sum(parts.astype(jnp.float32), axis=0) * (1.0 / QUERY_SCALE)
    query = spread(query.astype(jnp.bfloat16), "z").reshape(tokens, width // CORES)

    rows = width // shards
    pieces = attend(query, here, there, keys.shape[1], chips).astype(jnp.float16)
    pieces = lax.all_to_all(pieces, "z", 0, 0).astype(jnp.float32)
    level = (
        pieces[:, rows, :] * LEVEL_STEP
        + pieces[:, rows + 1, :]
        + pieces[:, rows + 2, :] * (1.0 / LEVEL_STEP)
    )
    factor = jnp.exp2(level - jnp.max(level, axis=0, keepdims=True))
    numer = jnp.sum(pieces[:, :rows, :] * factor[:, None, :], axis=0)
    denom = jnp.sum(factor, axis=0, keepdims=True) * ACCUM_SCALE
    attended = spread((numer / denom).astype(jnp.bfloat16), ("core", "z")).reshape(width, tokens)

    projected = lax.dot_general(
        attended, w_out[0], (((0,), (0,)), ((), ())), preferred_element_type=jnp.float32
    )
    projected = (projected * OUT_SCALE).astype(jnp.float16).reshape(heads, step, -1)
    parts = lax.all_to_all(projected, "tp", 0, 0).astype(jnp.float32)
    updated = (own.astype(jnp.float32) + jnp.sum(parts, axis=0) * (1.0 / OUT_SCALE)).astype(jnp.bfloat16)
    return from_behind(updated, "section", 1)[None]


def solution(mesh):
    shards, sections, heads = (mesh.shape[name] for name in ("kvp", "section", "tp"))
    split = Mesh(
        mesh.devices.reshape(shards // CORES, CORES, sections, heads),
        ("z", "core", "section", "tp"),
    )
    shard = ("z", "core")
    in_specs = (
        P("section", "tp", shard),
        P("section", shard),
        P("section", shard, "tp"),
        P("section", shard, "tp", None),
        P("section", shard, "tp", None),
        P(shard),
        P("section", "tp", shard),
    )
    out_specs = P("section", "tp", shard)
    return jax.shard_map(local, mesh=split, in_specs=in_specs, out_specs=out_specs, check_vma=False)
```

time: 270 us -> 118 us (0.44)
  the two profiles are of different devices: /device:TPU:8 before, /device:TPU:64 now
where the time goes in v1:
time: 118 us; the launch traced here: 117 us
  blocking collectives  81.2 us (69%)
  starting transfers between devices  15.3 us (13%)
  Pallas kernels  7.84 us (7%)
  waiting for transfers between devices  6.04 us (5%)
  local copies, waits for them, and re-layouts  5.15 us (4%)
    all_to_all x2, blocking collectives, spread(): lax.all_to_all(jnp.broadcast_to(value[None], (count,) + value.shape), axi...  26.1 us
    all_to_all x1, blocking collectives, local(): normed = lax.all_to_all(normed, 'tp', 0, 0).reshape(tokens, -1)  16.6 us
    all_to_all x1, blocking collectives, local(): parts = lax.all_to_all(partial.astype(jnp.float16), ('core', 'z'), 0, 0)  15.4 us
    all_to_all x1, blocking collectives, local(): pieces = lax.all_to_all(pieces, 'z', 0, 0).astype(jnp.float32)  11.6 us
    all_to_all x1, blocking collectives, local(): parts = lax.all_to_all(projected, 'tp', 0, 0).astype(jnp.float32)  11.5 us
    all_to_all x1, starting transfers between devices, local(): squares = lax.all_to_all(squares, ('core', 'z'), 0, 0)  9.98 us
    pallas_call x1, Pallas kernels, attend(): pl.pallas_call(functools.partial(attend_kernel, chunks=chunks), out_shape...  6.27 us
    ppermute x2, starting transfers between devices, from_behind(): return lax.ppermute(value, axis, pairs)  5.31 us
  transfers between devices with their start and end apart: 3, of which 2 were waited for; matrix products, arithmetic and copies ran while one was open for 0% of the time, Pallas kernels for 1%

profile of v1, /device:TPU:64, one launch (start us, length us, event | category | flops | bytes accessed | tf_op | source)
XLA Modules:
  0.0 117.0 jit_solution(16643994550355711121)
XLA Ops:
  0.0 0.0 copy-start
  0.0 0.0 copy-start.4
  0.0 0.8 copy-done.4
  0.8 0.0 copy-start.5
  0.8 0.0 copy-start.6
  0.8 0.7 shard_map.73.after
  1.5 10.0 %all-to-all-start = ((f32[16,1,128]{2,1,0:T(1,128)}), f32[16,1,128]{2,1,0:T(1,128)S(1)}, u32[]{:S(2)}, u32[]{:S(2)}) async-start(f32[16,1,128]{2,1,0:T(1,128)} %shard_map.73.after), calls=%async_computation | async-start | bytes 16384 | tf_op jit(solution)/shard_map/all_to_all | solution.py:265
  12.1 0.0 copy-start.1
  12.2 1.2 %copy-done.1 = bf16[1,4096,1,128]{3,1,2,0:T(8,128)(2,1)S(1)} copy-done((bf16[1,4096,1,128]{3,1,2,0:T(8,128)(2,1)S(1)}, bf16[1,4096,1,128]{3,1,2,0:T(8,128)(2,1)}, u32[]{:S(2)}) %copy-start.1) | copy-done | bytes 1048600
  13.4 0.0 copy-start.2
  13.4 1.2 %copy-done.2 = bf16[1,4096,1,128]{3,1,2,0:T(8,128)(2,1)S(1)} copy-done((bf16[1,4096,1,128]{3,1,2,0:T(8,128)(2,1)S(1)}, bf16[1,4096,1,128]{3,1,2,0:T(8,128)(2,1)}, u32[]{:S(2)}) %copy-start.2) | copy-done | bytes 1048600
  14.6 0.5 shard_map.74.here
  15.1 2.6 %all-to-all-done.squares = f32[16,1,128]{2,1,0:T(1,128)S(1)} async-done(((f32[16,1,128]{2,1,0:T(1,128)}), f32[16,1,128]{2,1,0:T(1,128)S(1)}, u32[]{:S(2)}, u32[]{:S(2)}) %all-to-all-start) | async-done | bytes 8224 | tf_op jit(solution)/shard_map/all_to_all | solution.py:265
  17.7 1.9 %collective-permute-start = (bf16[8704,128]{1,0:T(8,128)(2,1)S(1)}, bf16[8704,128]{1,0:T(8,128)(2,1)S(1)}, u32[]{:S(2)}, u32[]{:S(2)}) collective-permute-start(bf16[8704,128]{1,0:T(8,128)(2,1)S(1)} %shard_map.74.here), channel_id=1, source_target_pairs={{0,32},{32,0},{1,33},{33,1},{2,34},{34,2},{3,35},{35,3},{4,36},{36... | collective-permute-start | bytes 6684680 | tf_op jit(solution)/shard_map/ppermute | solution.py:34
  19.6 0.0 copy-done.5
  19.6 0.0 copy-done.6
  19.6 0.1 shard_map.75
  19.7 16.6 %all_to_all.35 = bf16[8,16,512]{2,1,0:T(8,128)(2,1)S(1)} all-to-all(bf16[8,16,512]{2,1,0:T(8,128)(2,1)S(1)} %shard_map.75), channel_id=1, replica_groups=mesh['z'=8,'core'=2,'section'=4,'tp'=8] {'tp'}, dimensions={0} | all-to-all | bytes 262144 | tf_op jit(solution)/shard_map/all_to_all | solution.py:269
  36.4 0.0 copy-start.3
  36.4 1.2 %copy-done.3 = bf16[1,512,1024]{2,1,0:T(8,128)(2,1)S(1)} copy-done((bf16[1,512,1024]{2,1,0:T(8,128)(2,1)S(1)}, bf16[1,512,1024]{2,1,0:T(8,128)(2,1)}, u32[]{:S(2)}) %copy-start.3) | copy-done | bytes 1048600
  37.6 0.3 shard_map.76
  37.9 15.4 %all_to_all.36 = f16[16,16,512]{2,1,0:T(8,128)(2,1)S(1)} all-to-all(f16[16,16,512]{2,1,0:T(8,128)(2,1)S(1)} %convert_element_type.39), channel_id=1, replica_groups=mesh['z'=8,'core'=2,'section'=4,'tp'=8] {'core','z'}, dimensions={0} | all-to-all | bytes 524288 | tf_op jit(solution)/shard_map/all_to_all | solution.py:278
  53.4 11.2 %all_to_all.37 = bf16[8,16,512]{2,1,0:T(8,128)(2,1)S(1)} all-to-all(bf16[8,16,512]{2,1,0:T(8,128)(2,1)S(1)} %broadcast_in_dim.6), channel_id=1, replica_groups=mesh['z'=8,'core'=2,'section'=4,'tp'=8] {'z'}, dimensions={0} | all-to-all | bytes 262144 | tf_op jit(solution)/shard_map/all_to_all | solution.py:39
  64.6 0.0 collective-permute-done.there
  64.6 6.3 %shard_map.77 = f32[8,72,128]{2,1,0:T(8,128)S(1)} custom-call(bf16[128,512]{1,0:T(8,128)(2,1)S(1)} %bitcast.22, bf16[8704,128]{1,0:T(8,128)(2,1)S(1)} %shard_map.74.here, bf16[8704,128]{1,0:T(8,128)(2,1)S(1)} %collective-permute-done.there), custom_call_target="tpu_custom_call" | custom-call | flops 2147483648 | bytes 4194304 | tf_op jit(solution)/shard_map/pallas_call | solution.py:239
  70.9 11.6 %all_to_all.38 = f16[8,72,128]{2,1,0:T(8,128)(2,1)S(1)} all-to-all(f16[8,72,128]{2,1,0:T(8,128)(2,1)S(1)} %convert_element_type.42), channel_id=1, replica_groups=mesh['z'=8,'core'=2,'section'=4,'tp'=8] {'z'}, dimensions={0} | all-to-all | bytes 294912 | tf_op jit(solution)/shard_map/all_to_all | solution.py:284
  82.8 14.9 %all_to_all.39 = bf16[16,64,128]{2,1,0:T(8,128)(2,1)S(1)} all-to-all(bf16[16,64,128]{2,1,0:T(8,128)(2,1)S(1)} %broadcast_in_dim.7), channel_id=1, replica_groups=mesh['z'=8,'core'=2,'section'=4,'tp'=8] {'core','z'}, dimensions={0} | all-to-all | bytes 524288 | tf_op jit(solution)/shard_map/all_to_all | solution.py:39
  97.7 0.0 copy-done
  97.7 0.3 fusion
  98.0 11.5 %all_to_all.40 = f16[8,16,512]{2,1,0:T(8,128)(2,1)S(1)} all-to-all(f16[8,16,512]{2,1,0:T(8,128)(2,1)S(1)} %bitcast.24), channel_id=1, replica_groups=mesh['z'=8,'core'=2,'section'=4,'tp'=8] {'tp'}, dimensions={0} | all-to-all | bytes 262144 | tf_op jit(solution)/shard_map/all_to_all | solution.py:299
  109.5 3.4 %collective-permute-start.1 = (bf16[16,512]{1,0:T(8,128)(2,1)S(1)}, bf16[16,512]{1,0:T(8,128)(2,1)S(1)}, u32[]{:S(2)}, u32[]{:S(2)}) collective-permute-start(bf16[16,512]{1,0:T(8,128)(2,1)S(1)} %add_convert_fusion), channel_id=1, source_target_pairs={{0,8},{8,16},{16,24},{24,0},{1,9},{9,17},{17,25},{25,1},{2,10},{10... | collective-permute-start | bytes 49160 | tf_op jit(solution)/shard_map/ppermute | solution.py:34
  112.9 3.4 %collective-permute-done.1 = bf16[16,512]{1,0:T(8,128)(2,1)S(1)} collective-permute-done((bf16[16,512]{1,0:T(8,128)(2,1)S(1)}, bf16[16,512]{1,0:T(8,128)(2,1)S(1)}, u32[]{:S(2)}, u32[]{:S(2)}) %collective-permute-start.1) | collective-permute-done | bytes 16416 | tf_op jit(solution)/shard_map/ppermute | solution.py:34
  116.4 0.6 copy.10
  (15 shorter events, 0.3 us)
Async XLA Ops:
  0.0 97.7 %copy-start = (bf16[1,1024,512]{2,1,0:T(8,128)(2,1)S(1)}, bf16[1,1024,512]{2,1,0:T(8,128)(2,1)}, u32[]{:S(2)}) copy-start(bf16[1,1024,512]{2,1,0:T(8,128)(2,1)} %param.13) | copy-start | bytes 3145732
  0.0 0.8 copy-start.4
  0.8 18.8 %copy-start.5 = (bf16[1,16,512]{2,1,0:T(8,128)(2,1)S(1)}, bf16[1,16,512]{2,1,0:T(8,128)(2,1)}, u32[]{:S(2)}) copy-start(bf16[1,16,512]{2,1,0:T(8,128)(2,1)} %param.7) | copy-start | bytes 49156
  0.8 18.8 %copy-start.6 = (f32[1,512]{1,0:T(1,128)S(1)}, f32[1,512]{1,0:T(1,128)}, u32[]{:S(2)}) copy-start(f32[1,512]{1,0:T(1,128)} %gain.1) | copy-start | bytes 6148
  1.5 16.2 %all-to-all-start = ((f32[16,1,128]{2,1,0:T(1,128)}), f32[16,1,128]{2,1,0:T(1,128)S(1)}, u32[]{:S(2)}, u32[]{:S(2)}) async-start(f32[16,1,128]{2,1,0:T(1,128)} %shard_map.73.after), calls=%async_computation | async-start | bytes 16384 | tf_op jit(solution)/shard_map/all_to_all | solution.py:265
  12.1 1.2 %copy-start.1 = (bf16[1,4096,1,128]{3,1,2,0:T(8,128)(2,1)S(1)}, bf16[1,4096,1,128]{3,1,2,0:T(8,128)(2,1)}, u32[]{:S(2)}) copy-start(bf16[1,4096,1,128]{3,1,2,0:T(8,128)(2,1)} %param.10) | copy-start | bytes 3145732
  13.4 1.2 %copy-start.2 = (bf16[1,4096,1,128]{3,1,2,0:T(8,128)(2,1)S(1)}, bf16[1,4096,1,128]{3,1,2,0:T(8,128)(2,1)}, u32[]{:S(2)}) copy-start(bf16[1,4096,1,128]{3,1,2,0:T(8,128)(2,1)} %param.11) | copy-start | bytes 3145732
  17.7 47.0 %collective-permute-start = (bf16[8704,128]{1,0:T(8,128)(2,1)S(1)}, bf16[8704,128]{1,0:T(8,128)(2,1)S(1)}, u32[]{:S(2)}, u32[]{:S(2)}) collective-permute-start(bf16[8704,128]{1,0:T(8,128)(2,1)S(1)} %shard_map.74.here), channel_id=1, source_target_pairs={{0,32},{32,0},{1,33},{33,1},{2,34},{34,2},{3,35},{35,3},{4,36},{36... | collective-permute-start | bytes 6684680 | tf_op jit(solution)/shard_map/ppermute | solution.py:34
  36.4 1.2 %copy-start.3 = (bf16[1,512,1024]{2,1,0:T(8,128)(2,1)S(1)}, bf16[1,512,1024]{2,1,0:T(8,128)(2,1)}, u32[]{:S(2)}) copy-start(bf16[1,512,1024]{2,1,0:T(8,128)(2,1)} %param.9) | copy-start | bytes 3145732
  109.5 6.8 %collective-permute-start.1 = (bf16[16,512]{1,0:T(8,128)(2,1)S(1)}, bf16[16,512]{1,0:T(8,128)(2,1)S(1)}, u32[]{:S(2)}, u32[]{:S(2)}) collective-permute-start(bf16[16,512]{1,0:T(8,128)(2,1)S(1)} %add_convert_fusion), channel_id=1, source_target_pairs={{0,8},{8,16},{16,24},{24,0},{1,9},{9,17},{17,25},{25,1},{2,10},{10... | collective-permute-start | bytes 49160 | tf_op jit(solution)/shard_map/ppermute | solution.py:34

commit v2 on v1

--- a/solution.py
+++ b/solution.py
@@ -21,7 +21,8 @@
 STAT_ROWS = 8
 ONES_ROWS = 16
 VALUE_ROWS = HD + ONES_ROWS
-PIECE = 1024
+PIECE = 512
+REACH = 2048
 
 QUERY_SCALE = 128.0
 ACCUM_SCALE = 4096.0
@@ -58,18 +59,6 @@
     square = jnp.sum(jnp.where(at == lane, row, 0.0), axis=1, keepdims=True)
     normed = (wide * lax.rsqrt(square / D + EPS) * gain[...]).astype(jnp.bfloat16)
     out[...] = jnp.broadcast_to(normed[None], out.shape)
-
-
-def project_kernel(normed, weight, out, *, chips):
-    width = weight.shape[1] // CORES
-    step = normed.shape[0] // chips
-    for core in range(CORES):
-        part = jnp.dot(
-            normed[...],
-            weight[:, core * width : (core + 1) * width],
-            preferred_element_type=jnp.float32,
-        )
-        out[core * chips : (core + 1) * chips] = part.reshape(chips, step, width) * QUERY_SCALE
 
 
 def small_call(kernel, shape, dtype, *operands):
@@ -147,14 +136,19 @@
     )(lengths, keys, values, after)
 
 
-def attend_kernel(query, here, there, out, scores, *, chunks):
+def attend_kernel(query, here, there, out, scores, *, chunks, count):
     tokens = query.shape[0]
     wide = 2 * tokens
     cache = (here, there)
-    count = scores.shape[1]
-    pieces = count // PIECE
+    reach = scores.shape[1]
     pairs = OWN // 2
     unit = math.log2(math.e) / math.sqrt(HD)
+    units = [
+        (half, start, pair)
+        for half in range(CORES)
+        for start in range(0, count, reach)
+        for pair in range(pairs)
+    ]
 
     def query_pair(pair):
         base = pair * 2 * HD
@@ -162,54 +156,55 @@
             [query[:, base : base + HD], query[:, base + HD : base + 2 * HD]], axis=0
         )
 
-    def score_piece(number, pair_query, piece, top):
-        half, pair = divmod(number, pairs)
+    queries = [query_pair(pair) for pair in range(pairs)]
+
+    def score_piece(number, offset, top):
+        half, start, pair = units[number]
+        row = key_row(start + offset)
         part = lax.dot_general(
-            cache[half][key_row(piece * PIECE) : key_row(piece * PIECE) + PIECE, :],
-            pair_query,
+            cache[half][row : row + PIECE, :],
+            queries[pair],
             (((1,), (1,)), ((), ())),
             preferred_element_type=jnp.float32,
         )
-        scores[number % 2, piece * PIECE : (piece + 1) * PIECE, :] = part
+        scores[number % 2, offset : offset + PIECE, :] = part
         return jnp.maximum(top, jnp.max(part.reshape(PIECE // 8, 8, wide), axis=0))
 
-    first = jnp.full((8, wide), -jnp.inf, jnp.float32)
-    top = first
-    ahead = query_pair(0)
-    for piece in range(pieces):
-        top = score_piece(0, ahead, piece, top)
-    held = []
-    for number in range(CORES * pairs):
-        half, pair = divmod(number, pairs)
+    lowest = jnp.full((8, wide), -jnp.inf, jnp.float32)
+    top = lowest
+    for offset in range(0, reach, PIECE):
+        top = score_piece(0, offset, top)
+    held = [None] * pairs
+    for number, (half, start, pair) in enumerate(units):
         best = jnp.max(top, axis=0, keepdims=True)
-        top = first
-        more = number + 1 < CORES * pairs
-        if more:
-            ahead = query_pair((number + 1) % pairs)
+        top = lowest
         accum = jnp.zeros((VALUE_ROWS, wide), jnp.float32)
-        for piece in range(pieces):
-            if more:
-                top = score_piece(number + 1, ahead, piece, top)
-            span = slice(piece * PIECE, (piece + 1) * PIECE)
-            weight = jnp.exp2((scores[number % 2, span, :] - best) * unit).astype(jnp.bfloat16)
+        for offset in range(0, reach, PIECE):
+            if number + 1 < len(units):
+                top = score_piece(number + 1, offset, top)
+            weight = jnp.exp2((scores[number % 2, offset : offset + PIECE, :] - best) * unit)
             across = [
-                cache[half][value_row(start) : value_row(start) + VALUE_ROWS, :]
-                for start in range(piece * PIECE, (piece + 1) * PIECE, LANES)
+                cache[half][value_row(at) : value_row(at) + VALUE_ROWS, :]
+                for at in range(start + offset, start + offset + PIECE, LANES)
             ]
             accum += jnp.dot(
-                jnp.concatenate(across, axis=1), weight, preferred_element_type=jnp.float32
+                jnp.concatenate(across, axis=1),
+                weight.astype(jnp.bfloat16),
+                preferred_element_type=jnp.float32,
             )
-        held.append((best, accum))
-        if half + 1 < CORES:
-            continue
-
-        best_here, accum_here = held[pair]
-        both = jnp.maximum(best_here, best)
-        accum = accum_here * jnp.exp2((best_here - both) * unit) + accum * jnp.exp2(
-            (best - both) * unit
-        )
+        if held[pair] is not None:
+            before, summed = held[pair]
+            both = jnp.maximum(before, best)
+            accum = summed * jnp.exp2((before - both) * unit) + accum * jnp.exp2(
+                (best - both) * unit
+            )
+            best = both
+        held[pair] = (best, accum)
+
+    for pair in range(pairs):
+        best, accum = held[pair]
         total = accum[HD : HD + 1, :]
-        level = both * unit + jnp.log2(total)
+        level = best * unit + jnp.log2(total)
         high = jnp.where(jnp.abs(level) < 1.0, 0.0, level).astype(jnp.bfloat16).astype(jnp.float32)
         rest = level - high
         middle = rest.astype(jnp.bfloat16).astype(jnp.float32)
@@ -237,11 +232,11 @@
     tokens = query.shape[0]
     rows = OWN * HD // chunks
     return pl.pallas_call(
-        functools.partial(attend_kernel, chunks=chunks),
+        functools.partial(attend_kernel, chunks=chunks, count=count),
         out_shape=jax.ShapeDtypeStruct((chunks, rows + STAT_ROWS, tokens), jnp.float32),
         in_specs=[pl.BlockSpec(memory_space=pltpu.VMEM)] * 3,
         out_specs=pl.BlockSpec(memory_space=pltpu.VMEM),
-        scratch_shapes=[pltpu.VMEM((2, count, 2 * tokens), jnp.float32)],
+        scratch_shapes=[pltpu.VMEM((2, min(count, REACH), 2 * tokens), jnp.float32)],
         compiler_params=pltpu.CompilerParams(vmem_limit_bytes=24 * 1024 * 1024),
         cost_estimate=pl.CostEstimate(
             flops=4 * GROUP * tokens * count * HD,
@@ -268,14 +263,10 @@
     normed = small_call(norm_kernel, (heads,) + own.shape, jnp.bfloat16, squares, own, gain)
     normed = lax.all_to_all(normed, "tp", 0, 0).reshape(tokens, -1)
 
-    partial = small_call(
-        functools.partial(project_kernel, chips=chips),
-        (shards, tokens // chips, width // CORES),
-        jnp.float32,
-        normed,
-        w_query[0],
-    )
-    parts = lax.all_to_all(partial.astype(jnp.float16), ("core", "z"), 0, 0)
+    partial = jnp.dot(normed, w_query[0], preferred_element_type=jnp.float32) * QUERY_SCALE
+    partial = partial.astype(jnp.float16).reshape(tokens, CORES, width // CORES)
+    partial = jnp.swapaxes(partial, 0, 1).reshape(shards, tokens // chips, width // CORES)
+    parts = lax.all_to_all(partial, ("core", "z"), 0, 0)
     query = jnp.sum(parts.astype(jnp.float32), axis=0) * (1.0 / QUERY_SCALE)
     query = spread(query.astype(jnp.bfloat16), "z").reshape(tokens, width // CORES)
 

time: 118 us -> 116 us (0.983)
  local copies, waits for them, and re-layouts: 5.15 us -> 3.97 us
    unnamed x15, local copies, waits for them, and re-layouts: 5.09 us -> 3.87 us
  transfers between devices with their start and end apart: 3 -> 3, of which waited for: 2 -> 2; matrix products, arithmetic and copies ran while one was open for 0% -> 0% of each run, Pallas kernels for 1% -> 0%
where the time goes in v2:
time: 116 us; the launch traced here: 115 us
  blocking collectives  81.4 us (70%)
  starting transfers between devices  15.3 us (13%)
  Pallas kernels  7.1 us (6%)
  waiting for transfers between devices  6.04 us (5%)
  local copies, waits for them, and re-layouts  3.97 us (3%)
    all_to_all x2, blocking collectives, spread(): lax.all_to_all(jnp.broadcast_to(value[None], (count,) + value.shape), axi...  26.1 us
    all_to_all x1, blocking collectives, local(): normed = lax.all_to_all(normed, 'tp', 0, 0).reshape(tokens, -1)  16.6 us
    all_to_all x1, blocking collectives, local(): parts = lax.all_to_all(partial, ('core', 'z'), 0, 0)  15.4 us
    all_to_all x1, blocking collectives, local(): pieces = lax.all_to_all(pieces, 'z', 0, 0).astype(jnp.float32)  11.8 us
    all_to_all x1, blocking collectives, local(): parts = lax.all_to_all(projected, 'tp', 0, 0).astype(jnp.float32)  11.5 us
    all_to_all x1, starting transfers between devices, local(): squares = lax.all_to_all(squares, ('core', 'z'), 0, 0)  9.98 us
    pallas_call x1, Pallas kernels, attend(): pl.pallas_call(functools.partial(attend_kernel, chunks=chunks, count=coun...  5.84 us
    ppermute x2, starting transfers between devices, from_behind(): return lax.ppermute(value, axis, pairs)  5.31 us
  transfers between devices with their start and end apart: 3, of which 2 were waited for; matrix products, arithmetic and copies ran while one was open for 0% of the time, Pallas kernels for 0%

profile of v2, /device:TPU:64, one launch (start us, length us, event | category | flops | bytes accessed | tf_op | source)
XLA Modules:
  0.0 115.5 jit_solution(5392351422679991295)
XLA Ops:
  0.0 0.0 copy-start
  0.0 0.0 copy-start.3
  0.0 0.8 copy-done.3
  0.8 0.0 copy-start.4
  0.8 0.0 copy-start.5
  0.8 0.7 shard_map.73.after
  1.5 10.0 %all-to-all-start = ((f32[16,1,128]{2,1,0:T(1,128)}), f32[16,1,128]{2,1,0:T(1,128)S(1)}, u32[]{:S(2)}, u32[]{:S(2)}) async-start(f32[16,1,128]{2,1,0:T(1,128)} %shard_map.73.after), calls=%async_computation | async-start | bytes 16384 | tf_op jit(solution)/shard_map/all_to_all | solution.py:260
  12.1 0.0 copy-start.1
  12.2 1.2 %copy-done.1 = bf16[1,4096,1,128]{3,1,2,0:T(8,128)(2,1)S(1)} copy-done((bf16[1,4096,1,128]{3,1,2,0:T(8,128)(2,1)S(1)}, bf16[1,4096,1,128]{3,1,2,0:T(8,128)(2,1)}, u32[]{:S(2)}) %copy-start.1) | copy-done | bytes 1048600
  13.4 0.0 copy-start.2
  13.4 1.2 %copy-done.2 = bf16[1,4096,1,128]{3,1,2,0:T(8,128)(2,1)S(1)} copy-done((bf16[1,4096,1,128]{3,1,2,0:T(8,128)(2,1)S(1)}, bf16[1,4096,1,128]{3,1,2,0:T(8,128)(2,1)}, u32[]{:S(2)}) %copy-start.2) | copy-done | bytes 1048600
  14.6 0.5 shard_map.74.here
  15.1 2.6 %all-to-all-done.squares = f32[16,1,128]{2,1,0:T(1,128)S(1)} async-done(((f32[16,1,128]{2,1,0:T(1,128)}), f32[16,1,128]{2,1,0:T(1,128)S(1)}, u32[]{:S(2)}, u32[]{:S(2)}) %all-to-all-start) | async-done | bytes 8224 | tf_op jit(solution)/shard_map/all_to_all | solution.py:260
  17.7 1.9 %collective-permute-start = (bf16[8704,128]{1,0:T(8,128)(2,1)S(1)}, bf16[8704,128]{1,0:T(8,128)(2,1)S(1)}, u32[]{:S(2)}, u32[]{:S(2)}) collective-permute-start(bf16[8704,128]{1,0:T(8,128)(2,1)S(1)} %shard_map.74.here), channel_id=1, source_target_pairs={{0,32},{32,0},{1,33},{33,1},{2,34},{34,2},{3,35},{35,3},{4,36},{36... | collective-permute-start | bytes 6684680 | tf_op jit(solution)/shard_map/ppermute | solution.py:35
  19.6 0.0 copy-done.4
  19.6 0.0 copy-done.5
  19.6 0.1 shard_map.75
  19.7 16.6 %all_to_all.35 = bf16[8,16,512]{2,1,0:T(8,128)(2,1)S(1)} all-to-all(bf16[8,16,512]{2,1,0:T(8,128)(2,1)S(1)} %shard_map.75), channel_id=1, replica_groups=mesh['z'=8,'core'=2,'section'=4,'tp'=8] {'tp'}, dimensions={0} | all-to-all | bytes 262144 | tf_op jit(solution)/shard_map/all_to_all | solution.py:264
  36.4 0.0 copy-done
  36.4 0.3 fusion
  36.7 15.4 %all_to_all.36 = f16[16,16,512]{2,1,0:T(8,128)(2,1)S(1)} all-to-all(f16[16,16,512]{2,1,0:T(8,128)(2,1)S(1)} %bitcast.31), channel_id=1, replica_groups=mesh['z'=8,'core'=2,'section'=4,'tp'=8] {'core','z'}, dimensions={0} | all-to-all | bytes 524288 | tf_op jit(solution)/shard_map/all_to_all | solution.py:269
  52.2 11.2 %all_to_all.37 = bf16[8,16,512]{2,1,0:T(8,128)(2,1)S(1)} all-to-all(bf16[8,16,512]{2,1,0:T(8,128)(2,1)S(1)} %broadcast_in_dim.6), channel_id=1, replica_groups=mesh['z'=8,'core'=2,'section'=4,'tp'=8] {'z'}, dimensions={0} | all-to-all | bytes 262144 | tf_op jit(solution)/shard_map/all_to_all | solution.py:40
  63.4 0.0 collective-permute-done.there
  63.4 5.8 %shard_map.76 = f32[8,72,128]{2,1,0:T(8,128)S(1)} custom-call(bf16[128,512]{1,0:T(8,128)(2,1)S(1)} %bitcast.30, bf16[8704,128]{1,0:T(8,128)(2,1)S(1)} %shard_map.74.here, bf16[8704,128]{1,0:T(8,128)(2,1)S(1)} %collective-permute-done.there), custom_call_target="tpu_custom_call" | custom-call | flops 2147483648 | bytes 4194304 | tf_op jit(solution)/shard_map/pallas_call | solution.py:234
  69.3 0.0 copy-start.6
  69.3 11.8 %all_to_all.38 = f16[8,72,128]{2,1,0:T(8,128)(2,1)S(1)} all-to-all(f16[8,72,128]{2,1,0:T(8,128)(2,1)S(1)} %convert_element_type.42), channel_id=1, replica_groups=mesh['z'=8,'core'=2,'section'=4,'tp'=8] {'z'}, dimensions={0} | all-to-all | bytes 294912 | tf_op jit(solution)/shard_map/all_to_all | solution.py:275
  81.3 14.9 %all_to_all.39 = bf16[16,64,128]{2,1,0:T(8,128)(2,1)S(1)} all-to-all(bf16[16,64,128]{2,1,0:T(8,128)(2,1)S(1)} %broadcast_in_dim.7), channel_id=1, replica_groups=mesh['z'=8,'core'=2,'section'=4,'tp'=8] {'core','z'}, dimensions={0} | all-to-all | bytes 524288 | tf_op jit(solution)/shard_map/all_to_all | solution.py:40
  96.2 0.0 copy-done.6
  96.2 0.3 fusion.1
  96.5 11.5 %all_to_all.40 = f16[8,16,512]{2,1,0:T(8,128)(2,1)S(1)} all-to-all(f16[8,16,512]{2,1,0:T(8,128)(2,1)S(1)} %bitcast.35), channel_id=1, replica_groups=mesh['z'=8,'core'=2,'section'=4,'tp'=8] {'tp'}, dimensions={0} | all-to-all | bytes 262144 | tf_op jit(solution)/shard_map/all_to_all | solution.py:290
  108.0 3.4 %collective-permute-start.1 = (bf16[16,512]{1,0:T(8,128)(2,1)S(1)}, bf16[16,512]{1,0:T(8,128)(2,1)S(1)}, u32[]{:S(2)}, u32[]{:S(2)}) collective-permute-start(bf16[16,512]{1,0:T(8,128)(2,1)S(1)} %add_convert_fusion), channel_id=1, source_target_pairs={{0,8},{8,16},{16,24},{24,0},{1,9},{9,17},{17,25},{25,1},{2,10},{10... | collective-permute-start | bytes 49160 | tf_op jit(solution)/shard_map/ppermute | solution.py:35
  111.5 3.4 %collective-permute-done.1 = bf16[16,512]{1,0:T(8,128)(2,1)S(1)} collective-permute-done((bf16[16,512]{1,0:T(8,128)(2,1)S(1)}, bf16[16,512]{1,0:T(8,128)(2,1)S(1)}, u32[]{:S(2)}, u32[]{:S(2)}) %collective-permute-start.1) | collective-permute-done | bytes 16416 | tf_op jit(solution)/shard_map/ppermute | solution.py:35
  114.9 0.6 copy.14
  (15 shorter events, 0.3 us)
Async XLA Ops:
  0.0 36.4 %copy-start = (bf16[1,512,1024]{2,1,0:T(8,128)(2,1)S(1)}, bf16[1,512,1024]{2,1,0:T(8,128)(2,1)}, u32[]{:S(2)}) copy-start(bf16[1,512,1024]{2,1,0:T(8,128)(2,1)} %param.9) | copy-start | bytes 3145732
  0.0 0.8 copy-start.3
  0.8 18.8 %copy-start.4 = (bf16[1,16,512]{2,1,0:T(8,128)(2,1)S(1)}, bf16[1,16,512]{2,1,0:T(8,128)(2,1)}, u32[]{:S(2)}) copy-start(bf16[1,16,512]{2,1,0:T(8,128)(2,1)} %param.7) | copy-start | bytes 49156
  0.8 18.8 %copy-start.5 = (f32[1,512]{1,0:T(1,128)S(1)}, f32[1,512]{1,0:T(1,128)}, u32[]{:S(2)}) copy-start(f32[1,512]{1,0:T(1,128)} %gain.1) | copy-start | bytes 6148
  1.5 16.2 %all-to-all-start = ((f32[16,1,128]{2,1,0:T(1,128)}), f32[16,1,128]{2,1,0:T(1,128)S(1)}, u32[]{:S(2)}, u32[]{:S(2)}) async-start(f32[16,1,128]{2,1,0:T(1,128)} %shard_map.73.after), calls=%async_computation | async-start | bytes 16384 | tf_op jit(solution)/shard_map/all_to_all | solution.py:260
  12.1 1.2 %copy-start.1 = (bf16[1,4096,1,128]{3,1,2,0:T(8,128)(2,1)S(1)}, bf16[1,4096,1,128]{3,1,2,0:T(8,128)(2,1)}, u32[]{:S(2)}) copy-start(bf16[1,4096,1,128]{3,1,2,0:T(8,128)(2,1)} %param.10) | copy-start | bytes 3145732
  13.4 1.2 %copy-start.2 = (bf16[1,4096,1,128]{3,1,2,0:T(8,128)(2,1)S(1)}, bf16[1,4096,1,128]{3,1,2,0:T(8,128)(2,1)}, u32[]{:S(2)}) copy-start(bf16[1,4096,1,128]{3,1,2,0:T(8,128)(2,1)} %param.11) | copy-start | bytes 3145732
  17.7 45.8 %collective-permute-start = (bf16[8704,128]{1,0:T(8,128)(2,1)S(1)}, bf16[8704,128]{1,0:T(8,128)(2,1)S(1)}, u32[]{:S(2)}, u32[]{:S(2)}) collective-permute-start(bf16[8704,128]{1,0:T(8,128)(2,1)S(1)} %shard_map.74.here), channel_id=1, source_target_pairs={{0,32},{32,0},{1,33},{33,1},{2,34},{34,2},{3,35},{35,3},{4,36},{36... | collective-permute-start | bytes 6684680 | tf_op jit(solution)/shard_map/ppermute | solution.py:35
  69.3 26.9 %copy-start.6 = (bf16[1,1024,512]{2,1,0:T(8,128)(2,1)S(1)}, bf16[1,1024,512]{2,1,0:T(8,128)(2,1)}, u32[]{:S(2)}) copy-start(bf16[1,1024,512]{2,1,0:T(8,128)(2,1)} %param.13) | copy-start | bytes 3145732
  108.0 6.8 %collective-permute-start.1 = (bf16[16,512]{1,0:T(8,128)(2,1)S(1)}, bf16[16,512]{1,0:T(8,128)(2,1)S(1)}, u32[]{:S(2)}, u32[]{:S(2)}) collective-permute-start(bf16[16,512]{1,0:T(8,128)(2,1)S(1)} %add_convert_fusion), channel_id=1, source_target_pairs={{0,8},{8,16},{16,24},{24,0},{1,9},{9,17},{17,25},{25,1},{2,10},{10... | collective-permute-start | bytes 49160 | tf_op jit(solution)/shard_map/ppermute | solution.py:35

commit v3 on v2

--- a/solution.py
+++ b/solution.py
@@ -22,7 +22,7 @@
 ONES_ROWS = 16
 VALUE_ROWS = HD + ONES_ROWS
 PIECE = 512
-REACH = 2048
+REACH = 1024
 
 QUERY_SCALE = 128.0
 ACCUM_SCALE = 4096.0
@@ -40,25 +40,24 @@
     return lax.all_to_all(jnp.broadcast_to(value[None], (count,) + value.shape), axis, 0, 0)
 
 
-def square_kernel(span, out):
-    wide = span[...].astype(jnp.float32)
+def square_kernel(rows, out):
+    wide = rows[...].astype(jnp.float32)
     square = jnp.sum(wide * wide, axis=1, keepdims=True)
-    step = wide.shape[0]
-    at = lax.broadcasted_iota(jnp.int32, (step, LANES), 0)
-    lane = lax.broadcasted_iota(jnp.int32, (step, LANES), 1)
+    tokens = wide.shape[0]
+    at = lax.broadcasted_iota(jnp.int32, (tokens, tokens), 0)
+    lane = lax.broadcasted_iota(jnp.int32, (tokens, tokens), 1)
     row = jnp.sum(jnp.where(at == lane, square, 0.0), axis=0, keepdims=True)
     out[...] = jnp.broadcast_to(row[None], out.shape)
 
 
-def norm_kernel(squares, span, gain, out):
-    wide = span[...].astype(jnp.float32)
-    step = wide.shape[0]
+def norm_kernel(squares, rows, gain, out):
+    wide = rows[...].astype(jnp.float32)
+    tokens = wide.shape[0]
     row = jnp.sum(squares[...], axis=0)
-    at = lax.broadcasted_iota(jnp.int32, (step, LANES), 0)
-    lane = lax.broadcasted_iota(jnp.int32, (step, LANES), 1)
+    at = lax.broadcasted_iota(jnp.int32, (tokens, tokens), 0)
+    lane = lax.broadcasted_iota(jnp.int32, (tokens, tokens), 1)
     square = jnp.sum(jnp.where(at == lane, row, 0.0), axis=1, keepdims=True)
-    normed = (wide * lax.rsqrt(square / D + EPS) * gain[...]).astype(jnp.bfloat16)
-    out[...] = jnp.broadcast_to(normed[None], out.shape)
+    out[...] = (wide * lax.rsqrt(square / D + EPS) * gain[...]).astype(jnp.bfloat16)
 
 
 def small_call(kernel, shape, dtype, *operands):
@@ -81,8 +80,7 @@
     return key_row(step * PIECE) + PIECE + at // LANES * VALUE_ROWS
 
 
-def prepare_kernel(length, keys, values, after, out):
-    del after
+def prepare_kernel(length, keys, values, out):
     count = keys.shape[0]
     valid = length[0]
     at = lax.broadcasted_iota(jnp.int32, (HD, HD), 0)
@@ -117,7 +115,7 @@
     pl.when(valid < count)(functools.partial(write, True))
 
 
-def prepare(lengths, keys, values, after):
+def prepare(lengths, keys, values):
     count = keys.shape[0]
     return pl.pallas_call(
         prepare_kernel,
@@ -126,14 +124,13 @@
             pl.BlockSpec(memory_space=pltpu.SMEM),
             pl.BlockSpec(memory_space=pltpu.VMEM),
             pl.BlockSpec(memory_space=pltpu.VMEM),
-            pl.BlockSpec(memory_space=pl.ANY),
         ],
         out_specs=pl.BlockSpec(memory_space=pltpu.VMEM),
         compiler_params=pltpu.CompilerParams(vmem_limit_bytes=16 * 1024 * 1024),
         cost_estimate=pl.CostEstimate(
             flops=8 * count * HD, bytes_accessed=8 * count * HD, transcendentals=0
         ),
-    )(lengths, keys, values, after)
+    )(lengths, keys, values)
 
 
 def attend_kernel(query, here, there, out, scores, *, chunks, count):
@@ -255,14 +252,14 @@
     tokens = heads * step
     width = GROUP * HD
 
-    squares = small_call(square_kernel, (shards, 1, LANES), jnp.float32, own)
-    here = prepare(lengths, keys[0, :, 0, :], values[0, :, 0, :], squares)
+    here = prepare(lengths, keys[0, :, 0, :], values[0, :, 0, :])
+    span_rows = spread(own, "tp").reshape(tokens, -1)
+    span_rows, here = lax.optimization_barrier((span_rows, here))
+    there = from_behind(here, "core", 1)
+
+    squares = small_call(square_kernel, (shards, 1, tokens), jnp.float32, span_rows)
     squares = lax.all_to_all(squares, ("core", "z"), 0, 0)
-    squares, here = lax.optimization_barrier((squares, here))
-    there = from_behind(here, "core", 1)
-    normed = small_call(norm_kernel, (heads,) + own.shape, jnp.bfloat16, squares, own, gain)
-    normed = lax.all_to_all(normed, "tp", 0, 0).reshape(tokens, -1)
-
+    normed = small_call(norm_kernel, span_rows.shape, jnp.bfloat16, squares, span_rows, gain)
     partial = jnp.dot(normed, w_query[0], preferred_element_type=jnp.float32) * QUERY_SCALE
     partial = partial.astype(jnp.float16).reshape(tokens, CORES, width // CORES)
     partial = jnp.swapaxes(partial, 0, 1).reshape(shards, tokens // chips, width // CORES)

time: 116 us -> 115 us (level)
  waiting for transfers between devices: 6.04 us -> 8.96 us
  starting transfers between devices: 15.3 us -> 12.4 us
    all_to_all x1, waiting for transfers between devices: 2.6 us -> 5.52 us  [spread(): lax.all_to_all(jnp.broadcast_to(value[None], (count,) + value.shape), axi...]
    all_to_all x1, starting transfers between devices: 9.98 us -> 7.1 us  [spread(): lax.all_to_all(jnp.broadcast_to(value[None], (count,) + value.shape), axi...]
    broadcast_in_dim x2 -> x3, local copies, waits for them, and re-layouts: 0.05 us -> 1.51 us  [spread(): jnp.broadcast_to(value[None], (count,) + value.shape)]
    unnamed x15 -> x13, local copies, waits for them, and re-layouts: 3.87 us -> 3.07 us
  transfers between devices with their start and end apart: 3 -> 3, of which waited for: 2 -> 2; matrix products, arithmetic and copies ran while one was open for 0% -> 0% of each run, Pallas kernels for 0% -> 1%
where the time goes in v3:
time: 115 us
  blocking collectives  80.3 us (70%)
  starting transfers between devices  12.4 us (11%)
  waiting for transfers between devices  8.96 us (8%)
  Pallas kernels  6.77 us (6%)
  local copies, waits for them, and re-layouts  4.62 us (4%)
    all_to_all x2, blocking collectives, spread(): lax.all_to_all(jnp.broadcast_to(value[None], (count,) + value.shape), axi...  26.1 us
    all_to_all x1, blocking collectives, local(): squares = lax.all_to_all(squares, ('core', 'z'), 0, 0)  16.1 us
    all_to_all x1, blocking collectives, local(): parts = lax.all_to_all(partial, ('core', 'z'), 0, 0)  14.9 us
    all_to_all x1, blocking collectives, local(): pieces = lax.all_to_all(pieces, 'z', 0, 0).astype(jnp.float32)  11.8 us
    all_to_all x1, blocking collectives, local(): parts = lax.all_to_all(projected, 'tp', 0, 0).astype(jnp.float32)  11.5 us
    all_to_all x1, starting transfers between devices, spread(): lax.all_to_all(jnp.broadcast_to(value[None], (count,) + value.shape), axi...  7.1 us
    pallas_call x1, Pallas kernels, attend(): pl.pallas_call(functools.partial(attend_kernel, chunks=chunks, count=coun...  6.07 us
    all_to_all x1, waiting for transfers between devices, spread(): lax.all_to_all(jnp.broadcast_to(value[None], (count,) + value.shape), axi...  5.52 us
  transfers between devices with their start and end apart: 3, of which 2 were waited for; matrix products, arithmetic and copies ran while one was open for 0% of the time, Pallas kernels for 1%

profile of v3, /device:TPU:64, one launch (start us, length us, event | category | flops | bytes accessed | tf_op | source)
XLA Modules:
  0.0 114.8 jit_solution(1071357669324281114)
XLA Ops:
  0.0 0.0 copy-start
  0.0 1.5 %broadcast_in_dim.8 = bf16[8,16,512]{2,1,0:T(8,128)(2,1)} broadcast(bf16[16,512]{1,0:T(8,128)(2,1)} %bitcast.35), dimensions={1,2} | broadcast | bytes 147456 | tf_op jit(solution)/shard_map/broadcast_in_dim | solution.py:40
  1.5 7.1 %all-to-all-start = ((bf16[8,16,512]{2,1,0:T(8,128)(2,1)}), bf16[8,16,512]{2,1,0:T(8,128)(2,1)S(1)}, u32[]{:S(2)}, u32[]{:S(2)}) async-start(bf16[8,16,512]{2,1,0:T(8,128)(2,1)} %broadcast_in_dim.8), calls=%async_computation | async-start | bytes 262144 | tf_op jit(solution)/shard_map/all_to_all | solution.py:40
  9.2 0.0 copy-start.1
  9.2 1.2 %copy-done.1 = bf16[1,4096,1,128]{3,1,2,0:T(8,128)(2,1)S(1)} copy-done((bf16[1,4096,1,128]{3,1,2,0:T(8,128)(2,1)S(1)}, bf16[1,4096,1,128]{3,1,2,0:T(8,128)(2,1)}, u32[]{:S(2)}) %copy-start.1) | copy-done | bytes 1048600
  10.4 0.0 copy-start.2
  10.4 1.2 %copy-done.2 = bf16[1,4096,1,128]{3,1,2,0:T(8,128)(2,1)S(1)} copy-done((bf16[1,4096,1,128]{3,1,2,0:T(8,128)(2,1)S(1)}, bf16[1,4096,1,128]{3,1,2,0:T(8,128)(2,1)}, u32[]{:S(2)}) %copy-start.2) | copy-done | bytes 1048600
  11.7 0.0 copy-start.3
  11.7 0.5 shard_map.73.here
  12.1 5.5 %all-to-all-done = bf16[8,16,512]{2,1,0:T(8,128)(2,1)S(1)} async-done(((bf16[8,16,512]{2,1,0:T(8,128)(2,1)}), bf16[8,16,512]{2,1,0:T(8,128)(2,1)S(1)}, u32[]{:S(2)}, u32[]{:S(2)}) %all-to-all-start) | async-done | bytes 131104 | tf_op jit(solution)/shard_map/all_to_all | solution.py:40
  17.7 1.9 %collective-permute-start = (bf16[8704,128]{1,0:T(8,128)(2,1)S(1)}, bf16[8704,128]{1,0:T(8,128)(2,1)S(1)}, u32[]{:S(2)}, u32[]{:S(2)}) collective-permute-start(bf16[8704,128]{1,0:T(8,128)(2,1)S(1)} %shard_map.73.here), channel_id=1, source_target_pairs={{0,32},{32,0},{1,33},{33,1},{2,34},{34,2},{3,35},{35,3},{4,36},{36... | collective-permute-start | bytes 6684680 | tf_op jit(solution)/shard_map/ppermute | solution.py:35
  19.6 0.1 shard_map.74
  19.7 16.1 %all_to_all.35.squares = f32[16,1,128]{2,1,0:T(1,128)S(1)} all-to-all(f32[16,1,128]{2,1,0:T(1,128)S(1)} %shard_map.74), channel_id=1, replica_groups=mesh['z'=8,'core'=2,'section'=4,'tp'=8] {'core','z'}, dimensions={0} | all-to-all | bytes 16384 | tf_op jit(solution)/shard_map/all_to_all | solution.py:261
  35.8 0.0 copy-done.3
  35.8 0.1 shard_map.75
  36.0 0.0 copy-done
  36.0 0.3 fusion
  36.4 14.9 %all_to_all.36 = f16[16,16,512]{2,1,0:T(8,128)(2,1)S(1)} all-to-all(f16[16,16,512]{2,1,0:T(8,128)(2,1)S(1)} %bitcast.31), channel_id=1, replica_groups=mesh['z'=8,'core'=2,'section'=4,'tp'=8] {'core','z'}, dimensions={0} | all-to-all | bytes 524288 | tf_op jit(solution)/shard_map/all_to_all | solution.py:266
  51.3 11.2 %all_to_all.37 = bf16[8,16,512]{2,1,0:T(8,128)(2,1)S(1)} all-to-all(bf16[8,16,512]{2,1,0:T(8,128)(2,1)S(1)} %broadcast_in_dim.9), channel_id=1, replica_groups=mesh['z'=8,'core'=2,'section'=4,'tp'=8] {'z'}, dimensions={0} | all-to-all | bytes 262144 | tf_op jit(solution)/shard_map/all_to_all | solution.py:40
  62.5 0.0 collective-permute-done.there
  62.5 6.1 %shard_map.76 = f32[8,72,128]{2,1,0:T(8,128)S(1)} custom-call(bf16[128,512]{1,0:T(8,128)(2,1)S(1)} %bitcast.30, bf16[8704,128]{1,0:T(8,128)(2,1)S(1)} %shard_map.73.here, bf16[8704,128]{1,0:T(8,128)(2,1)S(1)} %collective-permute-done.there), custom_call_target="tpu_custom_call" | custom-call | flops 2147483648 | bytes 4194304 | tf_op jit(solution)/shard_map/pallas_call | solution.py:231
  68.5 0.0 copy-start.4
  68.6 0.0 copy-start.5
  68.6 11.8 %all_to_all.38 = f16[8,72,128]{2,1,0:T(8,128)(2,1)S(1)} all-to-all(f16[8,72,128]{2,1,0:T(8,128)(2,1)S(1)} %convert_element_type.42), channel_id=1, replica_groups=mesh['z'=8,'core'=2,'section'=4,'tp'=8] {'z'}, dimensions={0} | all-to-all | bytes 294912 | tf_op jit(solution)/shard_map/all_to_all | solution.py:272
  80.6 14.9 %all_to_all.39 = bf16[16,64,128]{2,1,0:T(8,128)(2,1)S(1)} all-to-all(bf16[16,64,128]{2,1,0:T(8,128)(2,1)S(1)} %broadcast_in_dim.10), channel_id=1, replica_groups=mesh['z'=8,'core'=2,'section'=4,'tp'=8] {'core','z'}, dimensions={0} | all-to-all | bytes 524288 | tf_op jit(solution)/shard_map/all_to_all | solution.py:40
  95.5 0.0 copy-done.4
  95.5 0.3 fusion.1
  95.8 11.5 %all_to_all.40 = f16[8,16,512]{2,1,0:T(8,128)(2,1)S(1)} all-to-all(f16[8,16,512]{2,1,0:T(8,128)(2,1)S(1)} %bitcast.34), channel_id=1, replica_groups=mesh['z'=8,'core'=2,'section'=4,'tp'=8] {'tp'}, dimensions={0} | all-to-all | bytes 262144 | tf_op jit(solution)/shard_map/all_to_all | solution.py:287
  107.3 0.0 copy-done.5
  107.4 3.4 %collective-permute-start.1 = (bf16[16,512]{1,0:T(8,128)(2,1)S(1)}, bf16[16,512]{1,0:T(8,128)(2,1)S(1)}, u32[]{:S(2)}, u32[]{:S(2)}) collective-permute-start(bf16[16,512]{1,0:T(8,128)(2,1)S(1)} %add_convert_fusion), channel_id=1, source_target_pairs={{0,8},{8,16},{16,24},{24,0},{1,9},{9,17},{17,25},{25,1},{2,10},{10... | collective-permute-start | bytes 49160 | tf_op jit(solution)/shard_map/ppermute | solution.py:35
  110.8 3.4 %collective-permute-done.1 = bf16[16,512]{1,0:T(8,128)(2,1)S(1)} collective-permute-done((bf16[16,512]{1,0:T(8,128)(2,1)S(1)}, bf16[16,512]{1,0:T(8,128)(2,1)S(1)}, u32[]{:S(2)}, u32[]{:S(2)}) %collective-permute-start.1) | collective-permute-done | bytes 16416 | tf_op jit(solution)/shard_map/ppermute | solution.py:35
  114.2 0.6 copy.14
  (15 shorter events, 0.3 us)
Async XLA Ops:
  0.0 36.0 %copy-start = (bf16[1,512,1024]{2,1,0:T(8,128)(2,1)S(1)}, bf16[1,512,1024]{2,1,0:T(8,128)(2,1)}, u32[]{:S(2)}) copy-start(bf16[1,512,1024]{2,1,0:T(8,128)(2,1)} %param.9) | copy-start | bytes 3145732
  1.5 16.2 %all-to-all-start = ((bf16[8,16,512]{2,1,0:T(8,128)(2,1)}), bf16[8,16,512]{2,1,0:T(8,128)(2,1)S(1)}, u32[]{:S(2)}, u32[]{:S(2)}) async-start(bf16[8,16,512]{2,1,0:T(8,128)(2,1)} %broadcast_in_dim.8), calls=%async_computation | async-start | bytes 262144 | tf_op jit(solution)/shard_map/all_to_all | solution.py:40
  9.2 1.2 %copy-start.1 = (bf16[1,4096,1,128]{3,1,2,0:T(8,128)(2,1)S(1)}, bf16[1,4096,1,128]{3,1,2,0:T(8,128)(2,1)}, u32[]{:S(2)}) copy-start(bf16[1,4096,1,128]{3,1,2,0:T(8,128)(2,1)} %param.10) | copy-start | bytes 3145732
  10.4 1.2 %copy-start.2 = (bf16[1,4096,1,128]{3,1,2,0:T(8,128)(2,1)S(1)}, bf16[1,4096,1,128]{3,1,2,0:T(8,128)(2,1)}, u32[]{:S(2)}) copy-start(bf16[1,4096,1,128]{3,1,2,0:T(8,128)(2,1)} %param.11) | copy-start | bytes 3145732
  11.7 24.2 %copy-start.3 = (f32[1,512]{1,0:T(1,128)S(1)}, f32[1,512]{1,0:T(1,128)}, u32[]{:S(2)}) copy-start(f32[1,512]{1,0:T(1,128)} %gain.1) | copy-start | bytes 6148
  17.7 44.8 %collective-permute-start = (bf16[8704,128]{1,0:T(8,128)(2,1)S(1)}, bf16[8704,128]{1,0:T(8,128)(2,1)S(1)}, u32[]{:S(2)}, u32[]{:S(2)}) collective-permute-start(bf16[8704,128]{1,0:T(8,128)(2,1)S(1)} %shard_map.73.here), channel_id=1, source_target_pairs={{0,32},{32,0},{1,33},{33,1},{2,34},{34,2},{3,35},{35,3},{4,36},{36... | collective-permute-start | bytes 6684680 | tf_op jit(solution)/shard_map/ppermute | solution.py:35
  68.5 27.0 %copy-start.4 = (bf16[1,1024,512]{2,1,0:T(8,128)(2,1)S(1)}, bf16[1,1024,512]{2,1,0:T(8,128)(2,1)}, u32[]{:S(2)}) copy-start(bf16[1,1024,512]{2,1,0:T(8,128)(2,1)} %param.13) | copy-start | bytes 3145732
  68.6 38.8 %copy-start.5 = (bf16[1,16,512]{2,1,0:T(8,128)(2,1)S(1)}, bf16[1,16,512]{2,1,0:T(8,128)(2,1)}, u32[]{:S(2)}) copy-start(bf16[1,16,512]{2,1,0:T(8,128)(2,1)} %param.7) | copy-start | bytes 49156
  107.4 6.8 %collective-permute-start.1 = (bf16[16,512]{1,0:T(8,128)(2,1)S(1)}, bf16[16,512]{1,0:T(8,128)(2,1)S(1)}, u32[]{:S(2)}, u32[]{:S(2)}) collective-permute-start(bf16[16,512]{1,0:T(8,128)(2,1)S(1)} %add_convert_fusion), channel_id=1, source_target_pairs={{0,8},{8,16},{16,24},{24,0},{1,9},{9,17},{17,25},{25,1},{2,10},{10... | collective-permute-start | bytes 49160 | tf_op jit(solution)/shard_map/ppermute | solution.py:35

commit v4 on v3

--- a/solution.py
+++ b/solution.py
@@ -21,8 +21,8 @@
 STAT_ROWS = 8
 ONES_ROWS = 16
 VALUE_ROWS = HD + ONES_ROWS
-PIECE = 512
-REACH = 1024
+PIECE = 2048
+REACH = 2048
 
 QUERY_SCALE = 128.0
 ACCUM_SCALE = 4096.0

time: 115 us -> 116 us (level)
  no operation moved by 1% of the time
where the time goes in v4:
time: 116 us; the launch traced here: 115 us
  blocking collectives  80.3 us (69%)
  starting transfers between devices  12.4 us (11%)
  waiting for transfers between devices  8.93 us (8%)
  Pallas kernels  7 us (6%)
  local copies, waits for them, and re-layouts  4.62 us (4%)
    all_to_all x2, blocking collectives, spread(): lax.all_to_all(jnp.broadcast_to(value[None], (count,) + value.shape), axi...  26.1 us
    all_to_all x1, blocking collectives, local(): squares = lax.all_to_all(squares, ('core', 'z'), 0, 0)  16.1 us
    all_to_all x1, blocking collectives, local(): parts = lax.all_to_all(partial, ('core', 'z'), 0, 0)  14.9 us
    all_to_all x1, blocking collectives, local(): pieces = lax.all_to_all(pieces, 'z', 0, 0).astype(jnp.float32)  11.8 us
    all_to_all x1, blocking collectives, local(): parts = lax.all_to_all(projected, 'tp', 0, 0).astype(jnp.float32)  11.5 us
    all_to_all x1, starting transfers between devices, spread(): lax.all_to_all(jnp.broadcast_to(value[None], (count,) + value.shape), axi...  7.1 us
    pallas_call x1, Pallas kernels, attend(): pl.pallas_call(functools.partial(attend_kernel, chunks=chunks, count=coun...  6.26 us
    all_to_all x1, waiting for transfers between devices, spread(): lax.all_to_all(jnp.broadcast_to(value[None], (count,) + value.shape), axi...  5.49 us
  transfers between devices with their start and end apart: 3, of which 2 were waited for; matrix products, arithmetic and copies ran while one was open for 0% of the time, Pallas kernels for 1%

profile of v4, /device:TPU:64, one launch (start us, length us, event | category | flops | bytes accessed | tf_op | source)
XLA Modules:
  0.0 115.0 jit_solution(11954519402329236514)
XLA Ops:
  0.0 0.0 copy-start
  0.0 1.5 %broadcast_in_dim.8 = bf16[8,16,512]{2,1,0:T(8,128)(2,1)} broadcast(bf16[16,512]{1,0:T(8,128)(2,1)} %bitcast.35), dimensions={1,2} | broadcast | bytes 147456 | tf_op jit(solution)/shard_map/broadcast_in_dim | solution.py:40
  1.5 7.1 %all-to-all-start = ((bf16[8,16,512]{2,1,0:T(8,128)(2,1)}), bf16[8,16,512]{2,1,0:T(8,128)(2,1)S(1)}, u32[]{:S(2)}, u32[]{:S(2)}) async-start(bf16[8,16,512]{2,1,0:T(8,128)(2,1)} %broadcast_in_dim.8), calls=%async_computation | async-start | bytes 262144 | tf_op jit(solution)/shard_map/all_to_all | solution.py:40
  9.2 0.0 copy-start.1
  9.2 1.2 %copy-done.1 = bf16[1,4096,1,128]{3,1,2,0:T(8,128)(2,1)S(1)} copy-done((bf16[1,4096,1,128]{3,1,2,0:T(8,128)(2,1)S(1)}, bf16[1,4096,1,128]{3,1,2,0:T(8,128)(2,1)}, u32[]{:S(2)}) %copy-start.1) | copy-done | bytes 1048600
  10.4 0.0 copy-start.2
  10.4 1.2 %copy-done.2 = bf16[1,4096,1,128]{3,1,2,0:T(8,128)(2,1)S(1)} copy-done((bf16[1,4096,1,128]{3,1,2,0:T(8,128)(2,1)S(1)}, bf16[1,4096,1,128]{3,1,2,0:T(8,128)(2,1)}, u32[]{:S(2)}) %copy-start.2) | copy-done | bytes 1048600
  11.7 0.0 copy-start.3
  11.7 0.5 shard_map.73.here
  12.2 5.5 %all-to-all-done = bf16[8,16,512]{2,1,0:T(8,128)(2,1)S(1)} async-done(((bf16[8,16,512]{2,1,0:T(8,128)(2,1)}), bf16[8,16,512]{2,1,0:T(8,128)(2,1)S(1)}, u32[]{:S(2)}, u32[]{:S(2)}) %all-to-all-start) | async-done | bytes 131104 | tf_op jit(solution)/shard_map/all_to_all | solution.py:40
  17.7 1.9 %collective-permute-start = (bf16[8704,128]{1,0:T(8,128)(2,1)S(1)}, bf16[8704,128]{1,0:T(8,128)(2,1)S(1)}, u32[]{:S(2)}, u32[]{:S(2)}) collective-permute-start(bf16[8704,128]{1,0:T(8,128)(2,1)S(1)} %shard_map.73.here), channel_id=1, source_target_pairs={{0,32},{32,0},{1,33},{33,1},{2,34},{34,2},{3,35},{35,3},{4,36},{36... | collective-permute-start | bytes 6684680 | tf_op jit(solution)/shard_map/ppermute | solution.py:35
  19.6 0.1 shard_map.74
  19.7 16.1 %all_to_all.35.squares = f32[16,1,128]{2,1,0:T(1,128)S(1)} all-to-all(f32[16,1,128]{2,1,0:T(1,128)S(1)} %shard_map.74), channel_id=1, replica_groups=mesh['z'=8,'core'=2,'section'=4,'tp'=8] {'core','z'}, dimensions={0} | all-to-all | bytes 16384 | tf_op jit(solution)/shard_map/all_to_all | solution.py:261
  35.8 0.0 copy-done.3
  35.8 0.1 shard_map.75
  36.0 0.0 copy-done
  36.0 0.3 fusion
  36.4 14.9 %all_to_all.36 = f16[16,16,512]{2,1,0:T(8,128)(2,1)S(1)} all-to-all(f16[16,16,512]{2,1,0:T(8,128)(2,1)S(1)} %bitcast.31), channel_id=1, replica_groups=mesh['z'=8,'core'=2,'section'=4,'tp'=8] {'core','z'}, dimensions={0} | all-to-all | bytes 524288 | tf_op jit(solution)/shard_map/all_to_all | solution.py:266
  51.3 11.2 %all_to_all.37 = bf16[8,16,512]{2,1,0:T(8,128)(2,1)S(1)} all-to-all(bf16[8,16,512]{2,1,0:T(8,128)(2,1)S(1)} %broadcast_in_dim.9), channel_id=1, replica_groups=mesh['z'=8,'core'=2,'section'=4,'tp'=8] {'z'}, dimensions={0} | all-to-all | bytes 262144 | tf_op jit(solution)/shard_map/all_to_all | solution.py:40
  62.5 0.0 collective-permute-done.there
  62.5 6.3 %shard_map.76 = f32[8,72,128]{2,1,0:T(8,128)S(1)} custom-call(bf16[128,512]{1,0:T(8,128)(2,1)S(1)} %bitcast.30, bf16[8704,128]{1,0:T(8,128)(2,1)S(1)} %shard_map.73.here, bf16[8704,128]{1,0:T(8,128)(2,1)S(1)} %collective-permute-done.there), custom_call_target="tpu_custom_call" | custom-call | flops 2147483648 | bytes 4194304 | tf_op jit(solution)/shard_map/pallas_call | solution.py:231
  68.7 0.0 copy-start.4
  68.8 0.0 copy-start.5
  68.8 11.8 %all_to_all.38 = f16[8,72,128]{2,1,0:T(8,128)(2,1)S(1)} all-to-all(f16[8,72,128]{2,1,0:T(8,128)(2,1)S(1)} %convert_element_type.42), channel_id=1, replica_groups=mesh['z'=8,'core'=2,'section'=4,'tp'=8] {'z'}, dimensions={0} | all-to-all | bytes 294912 | tf_op jit(solution)/shard_map/all_to_all | solution.py:272
  80.8 14.9 %all_to_all.39 = bf16[16,64,128]{2,1,0:T(8,128)(2,1)S(1)} all-to-all(bf16[16,64,128]{2,1,0:T(8,128)(2,1)S(1)} %broadcast_in_dim.10), channel_id=1, replica_groups=mesh['z'=8,'core'=2,'section'=4,'tp'=8] {'core','z'}, dimensions={0} | all-to-all | bytes 524288 | tf_op jit(solution)/shard_map/all_to_all | solution.py:40
  95.7 0.0 copy-done.4
  95.7 0.3 fusion.1
  96.0 11.5 %all_to_all.40 = f16[8,16,512]{2,1,0:T(8,128)(2,1)S(1)} all-to-all(f16[8,16,512]{2,1,0:T(8,128)(2,1)S(1)} %bitcast.34), channel_id=1, replica_groups=mesh['z'=8,'core'=2,'section'=4,'tp'=8] {'tp'}, dimensions={0} | all-to-all | bytes 262144 | tf_op jit(solution)/shard_map/all_to_all | solution.py:287
  107.5 0.0 copy-done.5
  107.6 3.4 %collective-permute-start.1 = (bf16[16,512]{1,0:T(8,128)(2,1)S(1)}, bf16[16,512]{1,0:T(8,128)(2,1)S(1)}, u32[]{:S(2)}, u32[]{:S(2)}) collective-permute-start(bf16[16,512]{1,0:T(8,128)(2,1)S(1)} %add_convert_fusion), channel_id=1, source_target_pairs={{0,8},{8,16},{16,24},{24,0},{1,9},{9,17},{17,25},{25,1},{2,10},{10... | collective-permute-start | bytes 49160 | tf_op jit(solution)/shard_map/ppermute | solution.py:35
  111.0 3.4 %collective-permute-done.1 = bf16[16,512]{1,0:T(8,128)(2,1)S(1)} collective-permute-done((bf16[16,512]{1,0:T(8,128)(2,1)S(1)}, bf16[16,512]{1,0:T(8,128)(2,1)S(1)}, u32[]{:S(2)}, u32[]{:S(2)}) %collective-permute-start.1) | collective-permute-done | bytes 16416 | tf_op jit(solution)/shard_map/ppermute | solution.py:35
  114.4 0.6 copy.14
  (15 shorter events, 0.3 us)
Async XLA Ops:
  0.0 36.0 %copy-start = (bf16[1,512,1024]{2,1,0:T(8,128)(2,1)S(1)}, bf16[1,512,1024]{2,1,0:T(8,128)(2,1)}, u32[]{:S(2)}) copy-start(bf16[1,512,1024]{2,1,0:T(8,128)(2,1)} %param.9) | copy-start | bytes 3145732
  1.5 16.2 %all-to-all-start = ((bf16[8,16,512]{2,1,0:T(8,128)(2,1)}), bf16[8,16,512]{2,1,0:T(8,128)(2,1)S(1)}, u32[]{:S(2)}, u32[]{:S(2)}) async-start(bf16[8,16,512]{2,1,0:T(8,128)(2,1)} %broadcast_in_dim.8), calls=%async_computation | async-start | bytes 262144 | tf_op jit(solution)/shard_map/all_to_all | solution.py:40
  9.2 1.2 %copy-start.1 = (bf16[1,4096,1,128]{3,1,2,0:T(8,128)(2,1)S(1)}, bf16[1,4096,1,128]{3,1,2,0:T(8,128)(2,1)}, u32[]{:S(2)}) copy-start(bf16[1,4096,1,128]{3,1,2,0:T(8,128)(2,1)} %param.10) | copy-start | bytes 3145732
  10.4 1.2 %copy-start.2 = (bf16[1,4096,1,128]{3,1,2,0:T(8,128)(2,1)S(1)}, bf16[1,4096,1,128]{3,1,2,0:T(8,128)(2,1)}, u32[]{:S(2)}) copy-start(bf16[1,4096,1,128]{3,1,2,0:T(8,128)(2,1)} %param.11) | copy-start | bytes 3145732
  11.7 24.2 %copy-start.3 = (f32[1,512]{1,0:T(1,128)S(1)}, f32[1,512]{1,0:T(1,128)}, u32[]{:S(2)}) copy-start(f32[1,512]{1,0:T(1,128)} %gain.1) | copy-start | bytes 6148
  17.7 44.8 %collective-permute-start = (bf16[8704,128]{1,0:T(8,128)(2,1)S(1)}, bf16[8704,128]{1,0:T(8,128)(2,1)S(1)}, u32[]{:S(2)}, u32[]{:S(2)}) collective-permute-start(bf16[8704,128]{1,0:T(8,128)(2,1)S(1)} %shard_map.73.here), channel_id=1, source_target_pairs={{0,32},{32,0},{1,33},{33,1},{2,34},{34,2},{3,35},{35,3},{4,36},{36... | collective-permute-start | bytes 6684680 | tf_op jit(solution)/shard_map/ppermute | solution.py:35
  68.7 27.0 %copy-start.4 = (bf16[1,1024,512]{2,1,0:T(8,128)(2,1)S(1)}, bf16[1,1024,512]{2,1,0:T(8,128)(2,1)}, u32[]{:S(2)}) copy-start(bf16[1,1024,512]{2,1,0:T(8,128)(2,1)} %param.13) | copy-start | bytes 3145732
  68.8 38.8 %copy-start.5 = (bf16[1,16,512]{2,1,0:T(8,128)(2,1)S(1)}, bf16[1,16,512]{2,1,0:T(8,128)(2,1)}, u32[]{:S(2)}) copy-start(bf16[1,16,512]{2,1,0:T(8,128)(2,1)} %param.7) | copy-start | bytes 49156
  107.6 6.8 %collective-permute-start.1 = (bf16[16,512]{1,0:T(8,128)(2,1)S(1)}, bf16[16,512]{1,0:T(8,128)(2,1)S(1)}, u32[]{:S(2)}, u32[]{:S(2)}) collective-permute-start(bf16[16,512]{1,0:T(8,128)(2,1)S(1)} %add_convert_fusion), channel_id=1, source_target_pairs={{0,8},{8,16},{16,24},{24,0},{1,9},{9,17},{17,25},{25,1},{2,10},{10... | collective-permute-start | bytes 49160 | tf_op jit(solution)/shard_map/ppermute | solution.py:35

commit v5 on v4

--- a/solution.py
+++ b/solution.py
@@ -21,7 +21,7 @@
 STAT_ROWS = 8
 ONES_ROWS = 16
 VALUE_ROWS = HD + ONES_ROWS
-PIECE = 2048
+PIECE = 1024
 REACH = 2048
 
 QUERY_SCALE = 128.0
@@ -175,7 +175,11 @@
     for number, (half, start, pair) in enumerate(units):
         best = jnp.max(top, axis=0, keepdims=True)
         top = lowest
-        accum = jnp.zeros((VALUE_ROWS, wide), jnp.float32)
+        accum = None
+        if held[pair] is not None:
+            before, accum = held[pair]
+            best = jnp.maximum(before, best)
+            accum = accum * jnp.exp2((before - best) * unit)
         for offset in range(0, reach, PIECE):
             if number + 1 < len(units):
                 top = score_piece(number + 1, offset, top)
@@ -184,18 +188,12 @@
                 cache[half][value_row(at) : value_row(at) + VALUE_ROWS, :]
                 for at in range(start + offset, start + offset + PIECE, LANES)
             ]
-            accum += jnp.dot(
+            product = jnp.dot(
                 jnp.concatenate(across, axis=1),
                 weight.astype(jnp.bfloat16),
                 preferred_element_type=jnp.float32,
             )
-        if held[pair] is not None:
-            before, summed = held[pair]
-            both = jnp.maximum(before, best)
-            accum = summed * jnp.exp2((before - both) * unit) + accum * jnp.exp2(
-                (best - both) * unit
-            )
-            best = both
+            accum = product if accum is None else accum + product
         held[pair] = (best, accum)
 
     for pair in range(pairs):

time: 116 us -> 116 us (level)
  no operation moved by 1% of the time
where the time goes in v5:
time: 116 us; the launch traced here: 115 us
  blocking collectives  80.3 us (69%)
  starting transfers between devices  12.4 us (11%)
  waiting for transfers between devices  8.96 us (8%)
  Pallas kernels  7.24 us (6%)
  local copies, waits for them, and re-layouts  4.62 us (4%)
    all_to_all x2, blocking collectives, spread(): lax.all_to_all(jnp.broadcast_to(value[None], (count,) + value.shape), axi...  26.1 us
    all_to_all x1, blocking collectives, local(): squares = lax.all_to_all(squares, ('core', 'z'), 0, 0)  16.1 us
    all_to_all x1, blocking collectives, local(): parts = lax.all_to_all(partial, ('core', 'z'), 0, 0)  14.9 us
    all_to_all x1, blocking collectives, local(): pieces = lax.all_to_all(pieces, 'z', 0, 0).astype(jnp.float32)  11.8 us
    all_to_all x1, blocking collectives, local(): parts = lax.all_to_all(projected, 'tp', 0, 0).astype(jnp.float32)  11.5 us
    all_to_all x1, starting transfers between devices, spread(): lax.all_to_all(jnp.broadcast_to(value[None], (count,) + value.shape), axi...  7.1 us
    pallas_call x1, Pallas kernels, attend(): pl.pallas_call(functools.partial(attend_kernel, chunks=chunks, count=coun...  6.53 us
    all_to_all x1, waiting for transfers between devices, spread(): lax.all_to_all(jnp.broadcast_to(value[None], (count,) + value.shape), axi...  5.52 us
  transfers between devices with their start and end apart: 3, of which 2 were waited for; matrix products, arithmetic and copies ran while one was open for 0% of the time, Pallas kernels for 1%

profile of v5, /device:TPU:64, one launch (start us, length us, event | category | flops | bytes accessed | tf_op | source)
XLA Modules:
  0.0 115.3 jit_solution(6581063072650598914)
XLA Ops:
  0.0 0.0 copy-start
  0.0 1.5 %broadcast_in_dim.8 = bf16[8,16,512]{2,1,0:T(8,128)(2,1)} broadcast(bf16[16,512]{1,0:T(8,128)(2,1)} %bitcast.35), dimensions={1,2} | broadcast | bytes 147456 | tf_op jit(solution)/shard_map/broadcast_in_dim | solution.py:40
  1.5 7.1 %all-to-all-start = ((bf16[8,16,512]{2,1,0:T(8,128)(2,1)}), bf16[8,16,512]{2,1,0:T(8,128)(2,1)S(1)}, u32[]{:S(2)}, u32[]{:S(2)}) async-start(bf16[8,16,512]{2,1,0:T(8,128)(2,1)} %broadcast_in_dim.8), calls=%async_computation | async-start | bytes 262144 | tf_op jit(solution)/shard_map/all_to_all | solution.py:40
  9.2 0.0 copy-start.1
  9.2 1.2 %copy-done.1 = bf16[1,4096,1,128]{3,1,2,0:T(8,128)(2,1)S(1)} copy-done((bf16[1,4096,1,128]{3,1,2,0:T(8,128)(2,1)S(1)}, bf16[1,4096,1,128]{3,1,2,0:T(8,128)(2,1)}, u32[]{:S(2)}) %copy-start.1) | copy-done | bytes 1048600
  10.4 0.0 copy-start.2
  10.4 1.2 %copy-done.2 = bf16[1,4096,1,128]{3,1,2,0:T(8,128)(2,1)S(1)} copy-done((bf16[1,4096,1,128]{3,1,2,0:T(8,128)(2,1)S(1)}, bf16[1,4096,1,128]{3,1,2,0:T(8,128)(2,1)}, u32[]{:S(2)}) %copy-start.2) | copy-done | bytes 1048600
  11.7 0.0 copy-start.3
  11.7 0.5 shard_map.73.here
  12.1 5.5 %all-to-all-done = bf16[8,16,512]{2,1,0:T(8,128)(2,1)S(1)} async-done(((bf16[8,16,512]{2,1,0:T(8,128)(2,1)}), bf16[8,16,512]{2,1,0:T(8,128)(2,1)S(1)}, u32[]{:S(2)}, u32[]{:S(2)}) %all-to-all-start) | async-done | bytes 131104 | tf_op jit(solution)/shard_map/all_to_all | solution.py:40
  17.7 1.9 %collective-permute-start = (bf16[8704,128]{1,0:T(8,128)(2,1)S(1)}, bf16[8704,128]{1,0:T(8,128)(2,1)S(1)}, u32[]{:S(2)}, u32[]{:S(2)}) collective-permute-start(bf16[8704,128]{1,0:T(8,128)(2,1)S(1)} %shard_map.73.here), channel_id=1, source_target_pairs={{0,32},{32,0},{1,33},{33,1},{2,34},{34,2},{3,35},{35,3},{4,36},{36... | collective-permute-start | bytes 6684680 | tf_op jit(solution)/shard_map/ppermute | solution.py:35
  19.6 0.1 shard_map.74
  19.7 16.1 %all_to_all.35.squares = f32[16,1,128]{2,1,0:T(1,128)S(1)} all-to-all(f32[16,1,128]{2,1,0:T(1,128)S(1)} %shard_map.74), channel_id=1, replica_groups=mesh['z'=8,'core'=2,'section'=4,'tp'=8] {'core','z'}, dimensions={0} | all-to-all | bytes 16384 | tf_op jit(solution)/shard_map/all_to_all | solution.py:259
  35.8 0.0 copy-done.3
  35.8 0.1 shard_map.75
  36.0 0.0 copy-done
  36.0 0.3 fusion
  36.4 14.9 %all_to_all.36 = f16[16,16,512]{2,1,0:T(8,128)(2,1)S(1)} all-to-all(f16[16,16,512]{2,1,0:T(8,128)(2,1)S(1)} %bitcast.31), channel_id=1, replica_groups=mesh['z'=8,'core'=2,'section'=4,'tp'=8] {'core','z'}, dimensions={0} | all-to-all | bytes 524288 | tf_op jit(solution)/shard_map/all_to_all | solution.py:264
  51.3 11.2 %all_to_all.37 = bf16[8,16,512]{2,1,0:T(8,128)(2,1)S(1)} all-to-all(bf16[8,16,512]{2,1,0:T(8,128)(2,1)S(1)} %broadcast_in_dim.9), channel_id=1, replica_groups=mesh['z'=8,'core'=2,'section'=4,'tp'=8] {'z'}, dimensions={0} | all-to-all | bytes 262144 | tf_op jit(solution)/shard_map/all_to_all | solution.py:40
  62.5 0.0 collective-permute-done.there
  62.5 6.5 %shard_map.76 = f32[8,72,128]{2,1,0:T(8,128)S(1)} custom-call(bf16[128,512]{1,0:T(8,128)(2,1)S(1)} %bitcast.30, bf16[8704,128]{1,0:T(8,128)(2,1)S(1)} %shard_map.73.here, bf16[8704,128]{1,0:T(8,128)(2,1)S(1)} %collective-permute-done.there), custom_call_target="tpu_custom_call" | custom-call | flops 2147483648 | bytes 4194304 | tf_op jit(solution)/shard_map/pallas_call | solution.py:229
  69.0 0.0 copy-start.4
  69.0 0.0 copy-start.5
  69.1 11.8 %all_to_all.38 = f16[8,72,128]{2,1,0:T(8,128)(2,1)S(1)} all-to-all(f16[8,72,128]{2,1,0:T(8,128)(2,1)S(1)} %convert_element_type.42), channel_id=1, replica_groups=mesh['z'=8,'core'=2,'section'=4,'tp'=8] {'z'}, dimensions={0} | all-to-all | bytes 294912 | tf_op jit(solution)/shard_map/all_to_all | solution.py:270
  81.1 14.9 %all_to_all.39 = bf16[16,64,128]{2,1,0:T(8,128)(2,1)S(1)} all-to-all(bf16[16,64,128]{2,1,0:T(8,128)(2,1)S(1)} %broadcast_in_dim.10), channel_id=1, replica_groups=mesh['z'=8,'core'=2,'section'=4,'tp'=8] {'core','z'}, dimensions={0} | all-to-all | bytes 524288 | tf_op jit(solution)/shard_map/all_to_all | solution.py:40
  96.0 0.0 copy-done.4
  96.0 0.3 fusion.1
  96.3 11.5 %all_to_all.40 = f16[8,16,512]{2,1,0:T(8,128)(2,1)S(1)} all-to-all(f16[8,16,512]{2,1,0:T(8,128)(2,1)S(1)} %bitcast.34), channel_id=1, replica_groups=mesh['z'=8,'core'=2,'section'=4,'tp'=8] {'tp'}, dimensions={0} | all-to-all | bytes 262144 | tf_op jit(solution)/shard_map/all_to_all | solution.py:285
  107.8 0.0 copy-done.5
  107.8 3.4 %collective-permute-start.1 = (bf16[16,512]{1,0:T(8,128)(2,1)S(1)}, bf16[16,512]{1,0:T(8,128)(2,1)S(1)}, u32[]{:S(2)}, u32[]{:S(2)}) collective-permute-start(bf16[16,512]{1,0:T(8,128)(2,1)S(1)} %add_convert_fusion), channel_id=1, source_target_pairs={{0,8},{8,16},{16,24},{24,0},{1,9},{9,17},{17,25},{25,1},{2,10},{10... | collective-permute-start | bytes 49160 | tf_op jit(solution)/shard_map/ppermute | solution.py:35
  111.2 3.4 %collective-permute-done.1 = bf16[16,512]{1,0:T(8,128)(2,1)S(1)} collective-permute-done((bf16[16,512]{1,0:T(8,128)(2,1)S(1)}, bf16[16,512]{1,0:T(8,128)(2,1)S(1)}, u32[]{:S(2)}, u32[]{:S(2)}) %collective-permute-start.1) | collective-permute-done | bytes 16416 | tf_op jit(solution)/shard_map/ppermute | solution.py:35
  114.7 0.6 copy.14
  (15 shorter events, 0.3 us)
Async XLA Ops:
  0.0 36.0 %copy-start = (bf16[1,512,1024]{2,1,0:T(8,128)(2,1)S(1)}, bf16[1,512,1024]{2,1,0:T(8,128)(2,1)}, u32[]{:S(2)}) copy-start(bf16[1,512,1024]{2,1,0:T(8,128)(2,1)} %param.9) | copy-start | bytes 3145732
  1.5 16.2 %all-to-all-start = ((bf16[8,16,512]{2,1,0:T(8,128)(2,1)}), bf16[8,16,512]{2,1,0:T(8,128)(2,1)S(1)}, u32[]{:S(2)}, u32[]{:S(2)}) async-start(bf16[8,16,512]{2,1,0:T(8,128)(2,1)} %broadcast_in_dim.8), calls=%async_computation | async-start | bytes 262144 | tf_op jit(solution)/shard_map/all_to_all | solution.py:40
  9.2 1.2 %copy-start.1 = (bf16[1,4096,1,128]{3,1,2,0:T(8,128)(2,1)S(1)}, bf16[1,4096,1,128]{3,1,2,0:T(8,128)(2,1)}, u32[]{:S(2)}) copy-start(bf16[1,4096,1,128]{3,1,2,0:T(8,128)(2,1)} %param.10) | copy-start | bytes 3145732
  10.4 1.2 %copy-start.2 = (bf16[1,4096,1,128]{3,1,2,0:T(8,128)(2,1)S(1)}, bf16[1,4096,1,128]{3,1,2,0:T(8,128)(2,1)}, u32[]{:S(2)}) copy-start(bf16[1,4096,1,128]{3,1,2,0:T(8,128)(2,1)} %param.11) | copy-start | bytes 3145732
  11.7 24.2 %copy-start.3 = (f32[1,512]{1,0:T(1,128)S(1)}, f32[1,512]{1,0:T(1,128)}, u32[]{:S(2)}) copy-start(f32[1,512]{1,0:T(1,128)} %gain.1) | copy-start | bytes 6148
  17.7 44.8 %collective-permute-start = (bf16[8704,128]{1,0:T(8,128)(2,1)S(1)}, bf16[8704,128]{1,0:T(8,128)(2,1)S(1)}, u32[]{:S(2)}, u32[]{:S(2)}) collective-permute-start(bf16[8704,128]{1,0:T(8,128)(2,1)S(1)} %shard_map.73.here), channel_id=1, source_target_pairs={{0,32},{32,0},{1,33},{33,1},{2,34},{34,2},{3,35},{35,3},{4,36},{36... | collective-permute-start | bytes 6684680 | tf_op jit(solution)/shard_map/ppermute | solution.py:35
  69.0 27.0 %copy-start.4 = (bf16[1,1024,512]{2,1,0:T(8,128)(2,1)S(1)}, bf16[1,1024,512]{2,1,0:T(8,128)(2,1)}, u32[]{:S(2)}) copy-start(bf16[1,1024,512]{2,1,0:T(8,128)(2,1)} %param.13) | copy-start | bytes 3145732
  69.0 38.8 %copy-start.5 = (bf16[1,16,512]{2,1,0:T(8,128)(2,1)S(1)}, bf16[1,16,512]{2,1,0:T(8,128)(2,1)}, u32[]{:S(2)}) copy-start(bf16[1,16,512]{2,1,0:T(8,128)(2,1)} %param.7) | copy-start | bytes 49156
  107.8 6.8 %collective-permute-start.1 = (bf16[16,512]{1,0:T(8,128)(2,1)S(1)}, bf16[16,512]{1,0:T(8,128)(2,1)S(1)}, u32[]{:S(2)}, u32[]{:S(2)}) collective-permute-start(bf16[16,512]{1,0:T(8,128)(2,1)S(1)} %add_convert_fusion), channel_id=1, source_target_pairs={{0,8},{8,16},{16,24},{24,0},{1,9},{9,17},{17,25},{25,1},{2,10},{10... | collective-permute-start | bytes 49160 | tf_op jit(solution)/shard_map/ppermute | solution.py:35

commit v6 on v5

--- a/solution.py
+++ b/solution.py
@@ -171,15 +171,11 @@
     top = lowest
     for offset in range(0, reach, PIECE):
         top = score_piece(0, offset, top)
-    held = [None] * pairs
+    held = [[] for _ in range(pairs)]
     for number, (half, start, pair) in enumerate(units):
         best = jnp.max(top, axis=0, keepdims=True)
         top = lowest
         accum = None
-        if held[pair] is not None:
-            before, accum = held[pair]
-            best = jnp.maximum(before, best)
-            accum = accum * jnp.exp2((before - best) * unit)
         for offset in range(0, reach, PIECE):
             if number + 1 < len(units):
                 top = score_piece(number + 1, offset, top)
@@ -194,10 +190,11 @@
                 preferred_element_type=jnp.float32,
             )
             accum = product if accum is None else accum + product
-        held[pair] = (best, accum)
+        held[pair].append((best, accum))
 
     for pair in range(pairs):
-        best, accum = held[pair]
+        best = functools.reduce(jnp.maximum, [own for own, _ in held[pair]])
+        accum = sum(part * jnp.exp2((own - best) * unit) for own, part in held[pair])
         total = accum[HD : HD + 1, :]
         level = best * unit + jnp.log2(total)
         high = jnp.where(jnp.abs(level) < 1.0, 0.0, level).astype(jnp.bfloat16).astype(jnp.float32)

time: 116 us -> 115 us (level)
  no operation moved by 1% of the time
where the time goes in v6:
time: 115 us; the launch traced here: 114 us
  blocking collectives  80.3 us (70%)
  starting transfers between devices  12.4 us (11%)
  waiting for transfers between devices  8.96 us (8%)
  Pallas kernels  6.33 us (6%)
  local copies, waits for them, and re-layouts  4.62 us (4%)
    all_to_all x2, blocking collectives, spread(): lax.all_to_all(jnp.broadcast_to(value[None], (count,) + value.shape), axi...  26.1 us
    all_to_all x1, blocking collectives, local(): squares = lax.all_to_all(squares, ('core', 'z'), 0, 0)  16.1 us
    all_to_all x1, blocking collectives, local(): parts = lax.all_to_all(partial, ('core', 'z'), 0, 0)  14.9 us
    all_to_all x1, blocking collectives, local(): pieces = lax.all_to_all(pieces, 'z', 0, 0).astype(jnp.float32)  11.8 us
    all_to_all x1, blocking collectives, local(): parts = lax.all_to_all(projected, 'tp', 0, 0).astype(jnp.float32)  11.5 us
    all_to_all x1, starting transfers between devices, spread(): lax.all_to_all(jnp.broadcast_to(value[None], (count,) + value.shape), axi...  7.1 us
    pallas_call x1, Pallas kernels, attend(): pl.pallas_call(functools.partial(attend_kernel, chunks=chunks, count=coun...  5.62 us
    all_to_all x1, waiting for transfers between devices, spread(): lax.all_to_all(jnp.broadcast_to(value[None], (count,) + value.shape), axi...  5.52 us
  transfers between devices with their start and end apart: 3, of which 2 were waited for; matrix products, arithmetic and copies ran while one was open for 0% of the time, Pallas kernels for 1%

profile of v6, /device:TPU:64, one launch (start us, length us, event | category | flops | bytes accessed | tf_op | source)
XLA Modules:
  0.0 114.4 jit_solution(13787339021532164061)
XLA Ops:
  0.0 0.0 copy-start
  0.0 1.5 %broadcast_in_dim.8 = bf16[8,16,512]{2,1,0:T(8,128)(2,1)} broadcast(bf16[16,512]{1,0:T(8,128)(2,1)} %bitcast.35), dimensions={1,2} | broadcast | bytes 147456 | tf_op jit(solution)/shard_map/broadcast_in_dim | solution.py:40
  1.5 7.1 %all-to-all-start = ((bf16[8,16,512]{2,1,0:T(8,128)(2,1)}), bf16[8,16,512]{2,1,0:T(8,128)(2,1)S(1)}, u32[]{:S(2)}, u32[]{:S(2)}) async-start(bf16[8,16,512]{2,1,0:T(8,128)(2,1)} %broadcast_in_dim.8), calls=%async_computation | async-start | bytes 262144 | tf_op jit(solution)/shard_map/all_to_all | solution.py:40
  9.2 0.0 copy-start.1
  9.2 1.2 %copy-done.1 = bf16[1,4096,1,128]{3,1,2,0:T(8,128)(2,1)S(1)} copy-done((bf16[1,4096,1,128]{3,1,2,0:T(8,128)(2,1)S(1)}, bf16[1,4096,1,128]{3,1,2,0:T(8,128)(2,1)}, u32[]{:S(2)}) %copy-start.1) | copy-done | bytes 1048600
  10.4 0.0 copy-start.2
  10.4 1.2 %copy-done.2 = bf16[1,4096,1,128]{3,1,2,0:T(8,128)(2,1)S(1)} copy-done((bf16[1,4096,1,128]{3,1,2,0:T(8,128)(2,1)S(1)}, bf16[1,4096,1,128]{3,1,2,0:T(8,128)(2,1)}, u32[]{:S(2)}) %copy-start.2) | copy-done | bytes 1048600
  11.7 0.0 copy-start.3
  11.7 0.5 shard_map.73.here
  12.1 5.5 %all-to-all-done = bf16[8,16,512]{2,1,0:T(8,128)(2,1)S(1)} async-done(((bf16[8,16,512]{2,1,0:T(8,128)(2,1)}), bf16[8,16,512]{2,1,0:T(8,128)(2,1)S(1)}, u32[]{:S(2)}, u32[]{:S(2)}) %all-to-all-start) | async-done | bytes 131104 | tf_op jit(solution)/shard_map/all_to_all | solution.py:40
  17.7 1.9 %collective-permute-start = (bf16[8704,128]{1,0:T(8,128)(2,1)S(1)}, bf16[8704,128]{1,0:T(8,128)(2,1)S(1)}, u32[]{:S(2)}, u32[]{:S(2)}) collective-permute-start(bf16[8704,128]{1,0:T(8,128)(2,1)S(1)} %shard_map.73.here), channel_id=1, source_target_pairs={{0,32},{32,0},{1,33},{33,1},{2,34},{34,2},{3,35},{35,3},{4,36},{36... | collective-permute-start | bytes 6684680 | tf_op jit(solution)/shard_map/ppermute | solution.py:35
  19.6 0.1 shard_map.74
  19.7 16.1 %all_to_all.35.squares = f32[16,1,128]{2,1,0:T(1,128)S(1)} all-to-all(f32[16,1,128]{2,1,0:T(1,128)S(1)} %shard_map.74), channel_id=1, replica_groups=mesh['z'=8,'core'=2,'section'=4,'tp'=8] {'core','z'}, dimensions={0} | all-to-all | bytes 16384 | tf_op jit(solution)/shard_map/all_to_all | solution.py:256
  35.8 0.0 copy-done.3
  35.8 0.1 shard_map.75
  36.0 0.0 copy-done
  36.0 0.3 fusion
  36.4 14.9 %all_to_all.36 = f16[16,16,512]{2,1,0:T(8,128)(2,1)S(1)} all-to-all(f16[16,16,512]{2,1,0:T(8,128)(2,1)S(1)} %bitcast.31), channel_id=1, replica_groups=mesh['z'=8,'core'=2,'section'=4,'tp'=8] {'core','z'}, dimensions={0} | all-to-all | bytes 524288 | tf_op jit(solution)/shard_map/all_to_all | solution.py:261
  51.3 11.2 %all_to_all.37 = bf16[8,16,512]{2,1,0:T(8,128)(2,1)S(1)} all-to-all(bf16[8,16,512]{2,1,0:T(8,128)(2,1)S(1)} %broadcast_in_dim.9), channel_id=1, replica_groups=mesh['z'=8,'core'=2,'section'=4,'tp'=8] {'z'}, dimensions={0} | all-to-all | bytes 262144 | tf_op jit(solution)/shard_map/all_to_all | solution.py:40
  62.5 0.0 collective-permute-done.there
  62.5 5.6 %shard_map.76 = f32[8,72,128]{2,1,0:T(8,128)S(1)} custom-call(bf16[128,512]{1,0:T(8,128)(2,1)S(1)} %bitcast.30, bf16[8704,128]{1,0:T(8,128)(2,1)S(1)} %shard_map.73.here, bf16[8704,128]{1,0:T(8,128)(2,1)S(1)} %collective-permute-done.there), custom_call_target="tpu_custom_call" | custom-call | flops 2147483648 | bytes 4194304 | tf_op jit(solution)/shard_map/pallas_call | solution.py:226
  68.1 0.0 copy-start.4
  68.1 0.0 copy-start.5
  68.2 11.8 %all_to_all.38 = f16[8,72,128]{2,1,0:T(8,128)(2,1)S(1)} all-to-all(f16[8,72,128]{2,1,0:T(8,128)(2,1)S(1)} %convert_element_type.42), channel_id=1, replica_groups=mesh['z'=8,'core'=2,'section'=4,'tp'=8] {'z'}, dimensions={0} | all-to-all | bytes 294912 | tf_op jit(solution)/shard_map/all_to_all | solution.py:267
  80.2 14.9 %all_to_all.39 = bf16[16,64,128]{2,1,0:T(8,128)(2,1)S(1)} all-to-all(bf16[16,64,128]{2,1,0:T(8,128)(2,1)S(1)} %broadcast_in_dim.10), channel_id=1, replica_groups=mesh['z'=8,'core'=2,'section'=4,'tp'=8] {'core','z'}, dimensions={0} | all-to-all | bytes 524288 | tf_op jit(solution)/shard_map/all_to_all | solution.py:40
  95.1 0.0 copy-done.4
  95.1 0.3 fusion.1
  95.4 11.5 %all_to_all.40 = f16[8,16,512]{2,1,0:T(8,128)(2,1)S(1)} all-to-all(f16[8,16,512]{2,1,0:T(8,128)(2,1)S(1)} %bitcast.34), channel_id=1, replica_groups=mesh['z'=8,'core'=2,'section'=4,'tp'=8] {'tp'}, dimensions={0} | all-to-all | bytes 262144 | tf_op jit(solution)/shard_map/all_to_all | solution.py:282
  106.9 0.0 copy-done.5
  106.9 3.4 %collective-permute-start.1 = (bf16[16,512]{1,0:T(8,128)(2,1)S(1)}, bf16[16,512]{1,0:T(8,128)(2,1)S(1)}, u32[]{:S(2)}, u32[]{:S(2)}) collective-permute-start(bf16[16,512]{1,0:T(8,128)(2,1)S(1)} %add_convert_fusion), channel_id=1, source_target_pairs={{0,8},{8,16},{16,24},{24,0},{1,9},{9,17},{17,25},{25,1},{2,10},{10... | collective-permute-start | bytes 49160 | tf_op jit(solution)/shard_map/ppermute | solution.py:35
  110.3 3.4 %collective-permute-done.1 = bf16[16,512]{1,0:T(8,128)(2,1)S(1)} collective-permute-done((bf16[16,512]{1,0:T(8,128)(2,1)S(1)}, bf16[16,512]{1,0:T(8,128)(2,1)S(1)}, u32[]{:S(2)}, u32[]{:S(2)}) %collective-permute-start.1) | collective-permute-done | bytes 16416 | tf_op jit(solution)/shard_map/ppermute | solution.py:35
  113.8 0.6 copy.14
  (15 shorter events, 0.3 us)
Async XLA Ops:
  0.0 36.0 %copy-start = (bf16[1,512,1024]{2,1,0:T(8,128)(2,1)S(1)}, bf16[1,512,1024]{2,1,0:T(8,128)(2,1)}, u32[]{:S(2)}) copy-start(bf16[1,512,1024]{2,1,0:T(8,128)(2,1)} %param.9) | copy-start | bytes 3145732
  1.5 16.2 %all-to-all-start = ((bf16[8,16,512]{2,1,0:T(8,128)(2,1)}), bf16[8,16,512]{2,1,0:T(8,128)(2,1)S(1)}, u32[]{:S(2)}, u32[]{:S(2)}) async-start(bf16[8,16,512]{2,1,0:T(8,128)(2,1)} %broadcast_in_dim.8), calls=%async_computation | async-start | bytes 262144 | tf_op jit(solution)/shard_map/all_to_all | solution.py:40
  9.2 1.2 %copy-start.1 = (bf16[1,4096,1,128]{3,1,2,0:T(8,128)(2,1)S(1)}, bf16[1,4096,1,128]{3,1,2,0:T(8,128)(2,1)}, u32[]{:S(2)}) copy-start(bf16[1,4096,1,128]{3,1,2,0:T(8,128)(2,1)} %param.10) | copy-start | bytes 3145732
  10.4 1.2 %copy-start.2 = (bf16[1,4096,1,128]{3,1,2,0:T(8,128)(2,1)S(1)}, bf16[1,4096,1,128]{3,1,2,0:T(8,128)(2,1)}, u32[]{:S(2)}) copy-start(bf16[1,4096,1,128]{3,1,2,0:T(8,128)(2,1)} %param.11) | copy-start | bytes 3145732
  11.7 24.2 %copy-start.3 = (f32[1,512]{1,0:T(1,128)S(1)}, f32[1,512]{1,0:T(1,128)}, u32[]{:S(2)}) copy-start(f32[1,512]{1,0:T(1,128)} %gain.1) | copy-start | bytes 6148
  17.7 44.8 %collective-permute-start = (bf16[8704,128]{1,0:T(8,128)(2,1)S(1)}, bf16[8704,128]{1,0:T(8,128)(2,1)S(1)}, u32[]{:S(2)}, u32[]{:S(2)}) collective-permute-start(bf16[8704,128]{1,0:T(8,128)(2,1)S(1)} %shard_map.73.here), channel_id=1, source_target_pairs={{0,32},{32,0},{1,33},{33,1},{2,34},{34,2},{3,35},{35,3},{4,36},{36... | collective-permute-start | bytes 6684680 | tf_op jit(solution)/shard_map/ppermute | solution.py:35
  68.1 27.0 %copy-start.4 = (bf16[1,1024,512]{2,1,0:T(8,128)(2,1)S(1)}, bf16[1,1024,512]{2,1,0:T(8,128)(2,1)}, u32[]{:S(2)}) copy-start(bf16[1,1024,512]{2,1,0:T(8,128)(2,1)} %param.13) | copy-start | bytes 3145732
  68.1 38.8 %copy-start.5 = (bf16[1,16,512]{2,1,0:T(8,128)(2,1)S(1)}, bf16[1,16,512]{2,1,0:T(8,128)(2,1)}, u32[]{:S(2)}) copy-start(bf16[1,16,512]{2,1,0:T(8,128)(2,1)} %param.7) | copy-start | bytes 49156
  106.9 6.8 %collective-permute-start.1 = (bf16[16,512]{1,0:T(8,128)(2,1)S(1)}, bf16[16,512]{1,0:T(8,128)(2,1)S(1)}, u32[]{:S(2)}, u32[]{:S(2)}) collective-permute-start(bf16[16,512]{1,0:T(8,128)(2,1)S(1)} %add_convert_fusion), channel_id=1, source_target_pairs={{0,8},{8,16},{16,24},{24,0},{1,9},{9,17},{17,25},{25,1},{2,10},{10... | collective-permute-start | bytes 49160 | tf_op jit(solution)/shard_map/ppermute | solution.py:35

commit v7 on v6

--- a/solution.py
+++ b/solution.py
@@ -22,6 +22,7 @@
 ONES_ROWS = 16
 VALUE_ROWS = HD + ONES_ROWS
 PIECE = 1024
+STEP = PIECE // 2
 REACH = 2048
 
 QUERY_SCALE = 128.0
@@ -159,17 +160,17 @@
         half, start, pair = units[number]
         row = key_row(start + offset)
         part = lax.dot_general(
-            cache[half][row : row + PIECE, :],
+            cache[half][row : row + STEP, :],
             queries[pair],
             (((1,), (1,)), ((), ())),
             preferred_element_type=jnp.float32,
         )
-        scores[number % 2, offset : offset + PIECE, :] = part
-        return jnp.maximum(top, jnp.max(part.reshape(PIECE // 8, 8, wide), axis=0))
+        scores[number % 2, offset : offset + STEP, :] = part
+        return jnp.maximum(top, jnp.max(part.reshape(STEP // 8, 8, wide), axis=0))
 
     lowest = jnp.full((8, wide), -jnp.inf, jnp.float32)
     top = lowest
-    for offset in range(0, reach, PIECE):
+    for offset in range(0, reach, STEP):
         top = score_piece(0, offset, top)
     held = [[] for _ in range(pairs)]
     for number, (half, start, pair) in enumerate(units):
@@ -190,6 +191,8 @@
                 preferred_element_type=jnp.float32,
             )
             accum = product if accum is None else accum + product
+            if number + 1 < len(units):
+                top = score_piece(number + 1, offset + STEP, top)
         held[pair].append((best, accum))
 
     for pair in range(pairs):

time: 115 us -> 115 us (level)
  no operation moved by 1% of the time
where the time goes in v7:
time: 115 us
  blocking collectives  80.3 us (70%)
  starting transfers between devices  12.4 us (11%)
  waiting for transfers between devices  8.96 us (8%)
  Pallas kernels  6.72 us (6%)
  local copies, waits for them, and re-layouts  4.62 us (4%)
    all_to_all x2, blocking collectives, spread(): lax.all_to_all(jnp.broadcast_to(value[None], (count,) + value.shape), axi...  26.1 us
    all_to_all x1, blocking collectives, local(): squares = lax.all_to_all(squares, ('core', 'z'), 0, 0)  16.1 us
    all_to_all x1, blocking collectives, local(): parts = lax.all_to_all(partial, ('core', 'z'), 0, 0)  14.9 us
    all_to_all x1, blocking collectives, local(): pieces = lax.all_to_all(pieces, 'z', 0, 0).astype(jnp.float32)  11.8 us
    all_to_all x1, blocking collectives, local(): parts = lax.all_to_all(projected, 'tp', 0, 0).astype(jnp.float32)  11.5 us
    all_to_all x1, starting transfers between devices, spread(): lax.all_to_all(jnp.broadcast_to(value[None], (count,) + value.shape), axi...  7.1 us
    pallas_call x1, Pallas kernels, attend(): pl.pallas_call(functools.partial(attend_kernel, chunks=chunks, count=coun...  6.01 us
    all_to_all x1, waiting for transfers between devices, spread(): lax.all_to_all(jnp.broadcast_to(value[None], (count,) + value.shape), axi...  5.52 us
  transfers between devices with their start and end apart: 3, of which 2 were waited for; matrix products, arithmetic and copies ran while one was open for 0% of the time, Pallas kernels for 1%

profile of v7, /device:TPU:64, one launch (start us, length us, event | category | flops | bytes accessed | tf_op | source)
XLA Modules:
  0.0 114.8 jit_solution(10346622138443193900)
XLA Ops:
  0.0 0.0 copy-start
  0.0 1.5 %broadcast_in_dim.8 = bf16[8,16,512]{2,1,0:T(8,128)(2,1)} broadcast(bf16[16,512]{1,0:T(8,128)(2,1)} %bitcast.35), dimensions={1,2} | broadcast | bytes 147456 | tf_op jit(solution)/shard_map/broadcast_in_dim | solution.py:41
  1.5 7.1 %all-to-all-start = ((bf16[8,16,512]{2,1,0:T(8,128)(2,1)}), bf16[8,16,512]{2,1,0:T(8,128)(2,1)S(1)}, u32[]{:S(2)}, u32[]{:S(2)}) async-start(bf16[8,16,512]{2,1,0:T(8,128)(2,1)} %broadcast_in_dim.8), calls=%async_computation | async-start | bytes 262144 | tf_op jit(solution)/shard_map/all_to_all | solution.py:41
  9.2 0.0 copy-start.1
  9.2 1.2 %copy-done.1 = bf16[1,4096,1,128]{3,1,2,0:T(8,128)(2,1)S(1)} copy-done((bf16[1,4096,1,128]{3,1,2,0:T(8,128)(2,1)S(1)}, bf16[1,4096,1,128]{3,1,2,0:T(8,128)(2,1)}, u32[]{:S(2)}) %copy-start.1) | copy-done | bytes 1048600
  10.4 0.0 copy-start.2
  10.4 1.2 %copy-done.2 = bf16[1,4096,1,128]{3,1,2,0:T(8,128)(2,1)S(1)} copy-done((bf16[1,4096,1,128]{3,1,2,0:T(8,128)(2,1)S(1)}, bf16[1,4096,1,128]{3,1,2,0:T(8,128)(2,1)}, u32[]{:S(2)}) %copy-start.2) | copy-done | bytes 1048600
  11.7 0.0 copy-start.3
  11.7 0.5 shard_map.73.here
  12.1 5.5 %all-to-all-done = bf16[8,16,512]{2,1,0:T(8,128)(2,1)S(1)} async-done(((bf16[8,16,512]{2,1,0:T(8,128)(2,1)}), bf16[8,16,512]{2,1,0:T(8,128)(2,1)S(1)}, u32[]{:S(2)}, u32[]{:S(2)}) %all-to-all-start) | async-done | bytes 131104 | tf_op jit(solution)/shard_map/all_to_all | solution.py:41
  17.7 1.9 %collective-permute-start = (bf16[8704,128]{1,0:T(8,128)(2,1)S(1)}, bf16[8704,128]{1,0:T(8,128)(2,1)S(1)}, u32[]{:S(2)}, u32[]{:S(2)}) collective-permute-start(bf16[8704,128]{1,0:T(8,128)(2,1)S(1)} %shard_map.73.here), channel_id=1, source_target_pairs={{0,32},{32,0},{1,33},{33,1},{2,34},{34,2},{3,35},{35,3},{4,36},{36... | collective-permute-start | bytes 6684680 | tf_op jit(solution)/shard_map/ppermute | solution.py:36
  19.6 0.1 shard_map.74
  19.7 16.1 %all_to_all.35.squares = f32[16,1,128]{2,1,0:T(1,128)S(1)} all-to-all(f32[16,1,128]{2,1,0:T(1,128)S(1)} %shard_map.74), channel_id=1, replica_groups=mesh['z'=8,'core'=2,'section'=4,'tp'=8] {'core','z'}, dimensions={0} | all-to-all | bytes 16384 | tf_op jit(solution)/shard_map/all_to_all | solution.py:259
  35.8 0.0 copy-done.3
  35.8 0.1 shard_map.75
  36.0 0.0 copy-done
  36.0 0.3 fusion
  36.4 14.9 %all_to_all.36 = f16[16,16,512]{2,1,0:T(8,128)(2,1)S(1)} all-to-all(f16[16,16,512]{2,1,0:T(8,128)(2,1)S(1)} %bitcast.31), channel_id=1, replica_groups=mesh['z'=8,'core'=2,'section'=4,'tp'=8] {'core','z'}, dimensions={0} | all-to-all | bytes 524288 | tf_op jit(solution)/shard_map/all_to_all | solution.py:264
  51.3 11.2 %all_to_all.37 = bf16[8,16,512]{2,1,0:T(8,128)(2,1)S(1)} all-to-all(bf16[8,16,512]{2,1,0:T(8,128)(2,1)S(1)} %broadcast_in_dim.9), channel_id=1, replica_groups=mesh['z'=8,'core'=2,'section'=4,'tp'=8] {'z'}, dimensions={0} | all-to-all | bytes 262144 | tf_op jit(solution)/shard_map/all_to_all | solution.py:41
  62.5 0.0 collective-permute-done.there
  62.5 6.0 %shard_map.76 = f32[8,72,128]{2,1,0:T(8,128)S(1)} custom-call(bf16[128,512]{1,0:T(8,128)(2,1)S(1)} %bitcast.30, bf16[8704,128]{1,0:T(8,128)(2,1)S(1)} %shard_map.73.here, bf16[8704,128]{1,0:T(8,128)(2,1)S(1)} %collective-permute-done.there), custom_call_target="tpu_custom_call" | custom-call | flops 2147483648 | bytes 4194304 | tf_op jit(solution)/shard_map/pallas_call | solution.py:229
  68.5 0.0 copy-start.4
  68.5 0.0 copy-start.5
  68.5 11.8 %all_to_all.38 = f16[8,72,128]{2,1,0:T(8,128)(2,1)S(1)} all-to-all(f16[8,72,128]{2,1,0:T(8,128)(2,1)S(1)} %convert_element_type.42), channel_id=1, replica_groups=mesh['z'=8,'core'=2,'section'=4,'tp'=8] {'z'}, dimensions={0} | all-to-all | bytes 294912 | tf_op jit(solution)/shard_map/all_to_all | solution.py:270
  80.6 14.9 %all_to_all.39 = bf16[16,64,128]{2,1,0:T(8,128)(2,1)S(1)} all-to-all(bf16[16,64,128]{2,1,0:T(8,128)(2,1)S(1)} %broadcast_in_dim.10), channel_id=1, replica_groups=mesh['z'=8,'core'=2,'section'=4,'tp'=8] {'core','z'}, dimensions={0} | all-to-all | bytes 524288 | tf_op jit(solution)/shard_map/all_to_all | solution.py:41
  95.5 0.0 copy-done.4
  95.5 0.3 fusion.1
  95.8 11.5 %all_to_all.40 = f16[8,16,512]{2,1,0:T(8,128)(2,1)S(1)} all-to-all(f16[8,16,512]{2,1,0:T(8,128)(2,1)S(1)} %bitcast.34), channel_id=1, replica_groups=mesh['z'=8,'core'=2,'section'=4,'tp'=8] {'tp'}, dimensions={0} | all-to-all | bytes 262144 | tf_op jit(solution)/shard_map/all_to_all | solution.py:285
  107.3 0.0 copy-done.5
  107.3 3.4 %collective-permute-start.1 = (bf16[16,512]{1,0:T(8,128)(2,1)S(1)}, bf16[16,512]{1,0:T(8,128)(2,1)S(1)}, u32[]{:S(2)}, u32[]{:S(2)}) collective-permute-start(bf16[16,512]{1,0:T(8,128)(2,1)S(1)} %add_convert_fusion), channel_id=1, source_target_pairs={{0,8},{8,16},{16,24},{24,0},{1,9},{9,17},{17,25},{25,1},{2,10},{10... | collective-permute-start | bytes 49160 | tf_op jit(solution)/shard_map/ppermute | solution.py:36
  110.7 3.4 %collective-permute-done.1 = bf16[16,512]{1,0:T(8,128)(2,1)S(1)} collective-permute-done((bf16[16,512]{1,0:T(8,128)(2,1)S(1)}, bf16[16,512]{1,0:T(8,128)(2,1)S(1)}, u32[]{:S(2)}, u32[]{:S(2)}) %collective-permute-start.1) | collective-permute-done | bytes 16416 | tf_op jit(solution)/shard_map/ppermute | solution.py:36
  114.2 0.6 copy.14
  (15 shorter events, 0.3 us)
Async XLA Ops:
  0.0 36.0 %copy-start = (bf16[1,512,1024]{2,1,0:T(8,128)(2,1)S(1)}, bf16[1,512,1024]{2,1,0:T(8,128)(2,1)}, u32[]{:S(2)}) copy-start(bf16[1,512,1024]{2,1,0:T(8,128)(2,1)} %param.9) | copy-start | bytes 3145732
  1.5 16.2 %all-to-all-start = ((bf16[8,16,512]{2,1,0:T(8,128)(2,1)}), bf16[8,16,512]{2,1,0:T(8,128)(2,1)S(1)}, u32[]{:S(2)}, u32[]{:S(2)}) async-start(bf16[8,16,512]{2,1,0:T(8,128)(2,1)} %broadcast_in_dim.8), calls=%async_computation | async-start | bytes 262144 | tf_op jit(solution)/shard_map/all_to_all | solution.py:41
  9.2 1.2 %copy-start.1 = (bf16[1,4096,1,128]{3,1,2,0:T(8,128)(2,1)S(1)}, bf16[1,4096,1,128]{3,1,2,0:T(8,128)(2,1)}, u32[]{:S(2)}) copy-start(bf16[1,4096,1,128]{3,1,2,0:T(8,128)(2,1)} %param.10) | copy-start | bytes 3145732
  10.4 1.2 %copy-start.2 = (bf16[1,4096,1,128]{3,1,2,0:T(8,128)(2,1)S(1)}, bf16[1,4096,1,128]{3,1,2,0:T(8,128)(2,1)}, u32[]{:S(2)}) copy-start(bf16[1,4096,1,128]{3,1,2,0:T(8,128)(2,1)} %param.11) | copy-start | bytes 3145732
  11.7 24.2 %copy-start.3 = (f32[1,512]{1,0:T(1,128)S(1)}, f32[1,512]{1,0:T(1,128)}, u32[]{:S(2)}) copy-start(f32[1,512]{1,0:T(1,128)} %gain.1) | copy-start | bytes 6148
  17.7 44.8 %collective-permute-start = (bf16[8704,128]{1,0:T(8,128)(2,1)S(1)}, bf16[8704,128]{1,0:T(8,128)(2,1)S(1)}, u32[]{:S(2)}, u32[]{:S(2)}) collective-permute-start(bf16[8704,128]{1,0:T(8,128)(2,1)S(1)} %shard_map.73.here), channel_id=1, source_target_pairs={{0,32},{32,0},{1,33},{33,1},{2,34},{34,2},{3,35},{35,3},{4,36},{36... | collective-permute-start | bytes 6684680 | tf_op jit(solution)/shard_map/ppermute | solution.py:36
  68.5 27.0 %copy-start.4 = (bf16[1,1024,512]{2,1,0:T(8,128)(2,1)S(1)}, bf16[1,1024,512]{2,1,0:T(8,128)(2,1)}, u32[]{:S(2)}) copy-start(bf16[1,1024,512]{2,1,0:T(8,128)(2,1)} %param.13) | copy-start | bytes 3145732
  68.5 38.8 %copy-start.5 = (bf16[1,16,512]{2,1,0:T(8,128)(2,1)S(1)}, bf16[1,16,512]{2,1,0:T(8,128)(2,1)}, u32[]{:S(2)}) copy-start(bf16[1,16,512]{2,1,0:T(8,128)(2,1)} %param.7) | copy-start | bytes 49156
  107.3 6.8 %collective-permute-start.1 = (bf16[16,512]{1,0:T(8,128)(2,1)S(1)}, bf16[16,512]{1,0:T(8,128)(2,1)S(1)}, u32[]{:S(2)}, u32[]{:S(2)}) collective-permute-start(bf16[16,512]{1,0:T(8,128)(2,1)S(1)} %add_convert_fusion), channel_id=1, source_target_pairs={{0,8},{8,16},{16,24},{24,0},{1,9},{9,17},{17,25},{25,1},{2,10},{10... | collective-permute-start | bytes 49160 | tf_op jit(solution)/shard_map/ppermute | solution.py:36
